TPU v7x, 512 devices: a whole 4x4x16 slice. The times are simulated.
512 devices in a mesh: dp: 16 (over y, x_lo, core), mp: 32 (over z, x_hi).
Axes of the slice: x: 4 (x_hi: 2, x_lo: 2; x = x_hi * 2 + x_lo), y: 4, z: 16, core: 2. Of those that a mesh axis runs over, the one named last changes fastest.
Arguments:
- points: bfloat16 [16384, 1024], P('dp'), may hold values from -24 to 24
- fine_centroids: float32 [32768, 1024], P('mp', 'dp'), may hold values from -4 to 4
- coarse_centroids: float32 [4096, 1024], P('dp'), may hold values from -4 to 4
Outputs:
- new_fine: float32 [32768, 1024], P('mp', 'dp')
- new_coarse: float32 [4096, 1024], P('dp')
All inputs are finite; a program needn't handle non-finite values.
Results may differ from a plain program's by a relative error of at most 0.01.
Values may be sent and summed in bfloat16 or wider, within the bound.
No kernel may reach another device: no remote copies, remote signals or barrier semaphores. Data moves between devices by JAX's collectives and lax.ppermute only.
A program may use at most 64 MiB of HBM per device.

v0:
```python
import math

import jax
import jax.numpy as jnp
from jax import lax
from jax.sharding import PartitionSpec as P

PRIOR = 1.0


def contract_rows(left, right):
    return lax.dot_general(
        left, right, (((1,), (1,)), ((), ())), preferred_element_type=jnp.float32
    )


def contract_points(weights_b, values_b):
    return lax.dot_general(
        weights_b, values_b, (((0,), (0,)), ((), ())), preferred_element_type=jnp.float32
    )


def local(points, fine_centroids, coarse_centroids):
    scale = math.sqrt(points.shape[1])
    fine_b = fine_centroids.astype(jnp.bfloat16)
    shard_cols = lax.all_gather(fine_b, "dp", axis=1, tiled=True)
    products = contract_rows(points, shard_cols)
    square_norms = jnp.sum(jnp.square(shard_cols.astype(jnp.float32)), axis=1)
    products, square_norms = (products, square_norms)
    scores = (2.0 * products - square_norms[None, :]) / scale
    highest = lax.pmax(jnp.max(scores, axis=1), "mp")
    weights = jnp.exp(scores - highest[:, None])
    total = lax.psum(jnp.sum(weights, axis=1), "mp")
    assigned = weights / total[:, None]
    fine_counts = jnp.sum(assigned, axis=0)
    assigned_b = assigned.astype(jnp.bfloat16)
    own_rows = lax.psum_scatter(
        contract_points(assigned_b, points), "dp", scatter_dimension=0, tiled=True
    )
    own_sum = lax.all_to_all(own_rows, "dp", split_axis=1, concat_axis=0, tiled=True)
    fine_counts = lax.psum(fine_counts, "dp")
    new_fine = (own_sum + fine_centroids) / (fine_counts + PRIOR)[:, None]
    fine_points_b = lax.all_gather(new_fine.astype(jnp.bfloat16), "dp", axis=1, tiled=True)
    coarse_b = coarse_centroids.astype(jnp.bfloat16)
    coarse_norms = jnp.sum(jnp.square(coarse_b.astype(jnp.float32)), axis=1)
    coarse_scores = (2.0 * contract_rows(fine_points_b, coarse_b) - coarse_norms[None, :]) / scale
    coarse_high = lax.pmax(jnp.max(coarse_scores, axis=1), "dp")
    coarse_weights = jnp.exp(coarse_scores - coarse_high[:, None])
    coarse_total = lax.psum(jnp.sum(coarse_weights, axis=1), "dp")
    coarse_assigned = coarse_weights / coarse_total[:, None]
    coarse_counts = jnp.sum(coarse_assigned, axis=0)
    coarse_numer = contract_points(coarse_assigned.astype(jnp.bfloat16), fine_points_b)
    coarse_numer, coarse_counts = lax.psum((coarse_numer, coarse_counts), "mp")
    new_coarse = (coarse_numer + coarse_centroids) / (coarse_counts + PRIOR)[:, None]
    return (new_fine, new_coarse)


def solution(mesh):
    in_specs = (P("dp", None), P("mp", "dp"), P("dp", None))
    out_specs = (P("mp", "dp"), P("dp", None))
    return jax.shard_map(local, mesh=mesh, in_specs=in_specs, out_specs=out_specs, check_vma=False)
```

profile of v0, /device:TPU:8, one launch (start us, length us, event | category | flops | bytes accessed | tf_op | source)
XLA Modules:
  0.0 772.1 jit_solution(5821238306655619971)
XLA Ops:
  7.2 0.0 copy-start
  7.2 0.0 all-gather.3.cloned.1.call-start
  7.2 1.8 convert_element_type.21
  9.0 0.0 all-gather.3.cloned.1.call-update
  9.0 0.0 reduce-scatter.2.cloned.1.call-start
  9.1 47.4 %all-gather.3.cloned.1.call-done = bf16[1024,1024]{0,1:T(8,128)(2,1)} async-done(((bf16[1024,64]{0,1:T(8,128)(2,1)}), bf16[1024,1024]{0,1:T(8,128)(2,1)}) %all-gather.3.cloned.1.call-update) | async-done | bytes 2097168 | tf_op jit(solution)/shard_map/all_gather | solution.py:26
  56.4 2.1 multiply_reduce_fusion
  58.5 0.0 copy-done
  58.5 6.1 fusion.2
  64.6 78.1 %pmax.14 = f32[1024]{0:T(1024)S(1)} all-reduce(f32[1024]{0:T(1024)S(1)} %get-tuple-element.4), channel_id=1, replica_groups=mesh['dp'=16,'mp'=32] {'mp'}, use_global_device_ids=true, to_apply=%region_2.0 | all-reduce | flops 1024 | bytes 8192 | tf_op jit(solution)/shard_map/pmax | solution.py:31
  142.7 3.2 fusion.1
  145.9 72.0 %psum.35 = f32[1024]{0:T(1024)S(1)} all-reduce(f32[1024]{0:T(1024)S(1)} %fusion.1), channel_id=1, replica_groups=mesh['dp'=16,'mp'=32] {'mp'}, use_global_device_ids=true, to_apply=%region_4.0 | all-reduce | flops 1024 | bytes 8192 | tf_op jit(solution)/shard_map/psum | solution.py:33
  217.9 6.7 fusion.3
  224.6 0.0 reduce-scatter.2.cloned.1.call-update
  224.6 68.4 %reduce-scatter.2.cloned.1.call-done = f32[64,1024]{1,0:T(8,128)} async-done(((f32[1024,1024]{1,0:T(8,128)}), f32[64,1024]{1,0:T(8,128)}) %reduce-scatter.2.cloned.1.call-update) | async-done | bytes 262160 | tf_op jit(solution)/shard_map/reduce_scatter | solution.py:37
  293.0 1.1 all_to_all.14
  294.1 1.0 copy.9
  295.0 0.0 copy-start.1
  295.0 2.2 reshape.15
  297.2 10.8 %all-to-all-start = ((f32[16,1,4096]{2,1,0:T(1,128)}), f32[16,1,4096]{2,1,0:T(1,128)S(1)}, u32[]{:S(2)}, u32[]{:S(2)}) async-start(f32[16,1,4096]{2,1,0:T(1,128)} %reshape.15), calls=%async_computation.1 | async-start | bytes 524288 | tf_op jit(solution)/shard_map/all_to_all | solution.py:40
  308.0 0.0 all-gather.5.cloned.1.call-start
  308.0 3.5 fusion.14
  311.5 23.8 %psum.36 = f32[1024]{0:T(1024)S(1)} all-reduce(f32[1024]{0:T(1024)S(1)} %fusion.14), channel_id=1, replica_groups=mesh['dp'=16,'mp'=32] {'dp'}, use_global_device_ids=true, to_apply=%region_7.0 | all-reduce | flops 1024 | bytes 8192 | tf_op jit(solution)/shard_map/psum | solution.py:41
  335.4 0.0 all-to-all-done
  335.4 0.0 copy-start.2
  335.4 0.7 copy-done.2
  336.1 0.5 broadcast.10
  336.6 2.2 reduce
  338.8 1.0 reshape.16
  339.8 1.2 copy.7
  341.0 1.7 fusion.16
  342.8 0.0 all-gather.5.cloned.1.call-update
  342.8 0.0 all-reduce.2.cloned.1.call-start
  342.9 0.0 copy-done.1
  342.9 0.1 multiply_reduce_fusion.1
  343.0 46.3 %all-gather.5.cloned.1.call-done = bf16[1024,1024]{0,1:T(8,128)(2,1)} async-done(((bf16[1024,64]{0,1:T(8,128)(2,1)}), bf16[1024,1024]{0,1:T(8,128)(2,1)}) %all-gather.5.cloned.1.call-update) | async-done | bytes 2097168 | tf_op jit(solution)/shard_map/all_gather | solution.py:43
  389.3 3.3 fusion.17
  392.6 23.5 %pmax.15 = f32[1024]{0:T(1024)S(1)} all-reduce(f32[1024]{0:T(1024)S(1)} %get-tuple-element.6), channel_id=1, replica_groups=mesh['dp'=16,'mp'=32] {'dp'}, use_global_device_ids=true, to_apply=%region_10.0 | all-reduce | flops 1024 | bytes 8192 | tf_op jit(solution)/shard_map/pmax | solution.py:47
  416.2 1.4 fusion.8
  417.6 26.1 %psum.37 = f32[1024]{0:T(1024)S(1)} all-reduce(f32[1024]{0:T(1024)S(1)} %fusion.8), channel_id=1, replica_groups=mesh['dp'=16,'mp'=32] {'dp'}, use_global_device_ids=true, to_apply=%region_12.0 | all-reduce | flops 1024 | bytes 8192 | tf_op jit(solution)/shard_map/psum | solution.py:49
  443.7 3.7 fusion.9
  447.3 0.0 all-reduce.2.cloned.1.call-update
  447.4 1.5 fusion.11
  448.8 78.2 %psum.39 = f32[256]{0:T(256)S(1)} all-reduce(f32[256]{0:T(256)S(1)} %fusion.11), channel_id=1, replica_groups=mesh['dp'=16,'mp'=32] {'mp'}, use_global_device_ids=true, to_apply=%region_15.0 | all-reduce | flops 256 | bytes 2048 | tf_op jit(solution)/shard_map/psum | solution.py:53
  527.1 236.1 %all-reduce.2.cloned.1.call-done = f32[256,1024]{1,0:T(8,128)} async-done(((f32[256,1024]{1,0:T(8,128)}), f32[256,1024]{1,0:T(8,128)}) %all-reduce.2.cloned.1.call-update) | async-done | bytes 1048592 | tf_op jit(solution)/shard_map/psum | solution.py:53
  763.1 2.4 add_divide_fusion
  (2 shorter events, 0.0 us)
Async XLA Ops:
  7.2 51.3 %copy-start = (bf16[1024,1024]{1,0:T(8,128)(2,1)S(1)}, bf16[1024,1024]{1,0:T(8,128)(2,1)}, u32[]{:S(2)}) copy-start(bf16[1024,1024]{1,0:T(8,128)(2,1)} %param.3) | copy-start | bytes 6291460
  7.2 49.3 %all-gather.3.cloned.1.call-start = ((), (), s32[]{:S(2)}) async-start(), calls=%async_computation.2 | async-start | bytes 2228224 | tf_op jit(solution)/shard_map/all_gather | solution.py:26
  9.0 283.9 %reduce-scatter.2.cloned.1.call-start = ((), (), s32[]{:S(2)}) async-start(), calls=%async_computation.3 | async-start | bytes 4456448 | tf_op jit(solution)/shard_map/reduce_scatter | solution.py:37
  295.0 47.8 %copy-start.1 = (f32[256,1024]{1,0:T(8,128)S(1)}, f32[256,1024]{1,0:T(8,128)}, u32[]{:S(2)}) copy-start(f32[256,1024]{1,0:T(8,128)} %param.5) | copy-start | bytes 3145732
  297.2 38.2 %all-to-all-start = ((f32[16,1,4096]{2,1,0:T(1,128)}), f32[16,1,4096]{2,1,0:T(1,128)S(1)}, u32[]{:S(2)}, u32[]{:S(2)}) async-start(f32[16,1,4096]{2,1,0:T(1,128)} %reshape.15), calls=%async_computation.1 | async-start | bytes 524288 | tf_op jit(solution)/shard_map/all_to_all | solution.py:40
  308.0 81.4 %all-gather.5.cloned.1.call-start = ((), (), s32[]{:S(2)}) async-start(), calls=%async_computation.4 | async-start | bytes 2228224 | tf_op jit(solution)/shard_map/all_gather | solution.py:43
  335.4 0.7 copy-start.2
  342.8 420.3 %all-reduce.2.cloned.1.call-start = ((), (), s32[]{:S(2)}) async-start(), calls=%async_computation.5 | async-start | bytes 2097152 | tf_op jit(solution)/shard_map/psum | solution.py:53
Sparse Core Ops, SparseCore 0:
  10.7 45.6 all-gather.2
  224.7 68.1 reduce-scatter.1
  342.9 46.3 all-gather.4
  447.5 315.6 all-reduce.1
where the time goes:
time: 773 us; the launch traced here: 772 us
  waiting for transfers between devices  398 us (51%)
  blocking collectives  302 us (39%)
  other arithmetic  19.9 us (3%)
  matrix products  19.7 us (3%)
  between operations  13.8 us (2%)
  starting transfers between devices  11 us (1%)
    psum x1, waiting for transfers between devices, local(): coarse_numer, coarse_counts = lax.psum((coarse_numer, coarse_counts), 'mp')  236 us
    psum x1, blocking collectives, local(): coarse_numer, coarse_counts = lax.psum((coarse_numer, coarse_counts), 'mp')  78.2 us
    pmax x1, blocking collectives, local(): highest = lax.pmax(jnp.max(scores, axis=1), 'mp')  78.1 us
    psum x1, blocking collectives, local(): total = lax.psum(jnp.sum(weights, axis=1), 'mp')  72 us
    reduce_scatter x1, waiting for transfers between devices, local(): lax.psum_scatter(contract_points(assigned_b, points), 'dp', scatter_dimen...  68.4 us
    all_gather x1, waiting for transfers between devices, local(): shard_cols = lax.all_gather(fine_b, 'dp', axis=1, tiled=True)  47.4 us
    all_gather x1, waiting for transfers between devices, local(): lax.all_gather(new_fine.astype(jnp.bfloat16), 'dp', axis=1, tiled=True)  46.3 us
    psum x1, blocking collectives, local(): coarse_total = lax.psum(jnp.sum(coarse_weights, axis=1), 'dp')  26.1 us
  transfers between devices with their start and end apart: 5, of which 4 were waited for; matrix products, arithmetic and copies ran while one was open for 1% of the time, Pallas kernels for 0%

commit v1 on v0

v1 whole, which is shorter than its diff:
```python
import functools
import math

import jax
import jax.numpy as jnp
from jax import lax
from jax.experimental import pallas as pl
from jax.experimental.pallas import tpu as pltpu
from jax.sharding import Mesh, PartitionSpec as P

PRIOR = 1.0
F32, BF16 = jnp.float32, jnp.bfloat16
LANES = 128
PAIR = [(0, 1), (1, 0)]
CHIPS = ("y", "xl")
NEAR = ("zl", "xh")
CHIP_COUNT = 8
VMEM = pl.BlockSpec(memory_space=pltpu.VMEM)
SMEM = pl.BlockSpec(memory_space=pltpu.SMEM)
PARAMS = pltpu.CompilerParams(vmem_limit_bytes=24 * 1024 * 1024)


def shape_of(shape, dtype):
    return jax.ShapeDtypeStruct(shape, dtype)


def call(kernel, out_shape, scalars, arrays, scratch=(), cost=None):
    specs = [SMEM] * len(scalars) + [VMEM] * len(arrays)
    outs = jax.tree.map(lambda _: VMEM, out_shape)
    return pl.pallas_call(
        kernel, out_shape=out_shape, in_specs=specs, out_specs=outs,
        scratch_shapes=list(scratch), compiler_params=PARAMS, cost_estimate=cost,
    )(*scalars, *arrays)


def spread(block, axis, size):
    return exchange(jnp.broadcast_to(block[None], (size,) + block.shape), axis)


def exchange(blocks, axis):
    return lax.all_to_all(blocks, axis, split_axis=0, concat_axis=0, tiled=True)


def swap(block, axis):
    return lax.ppermute(block, axis, PAIR)


def to_row(column):
    return jnp.broadcast_to(column, (column.shape[0], LANES)).T[0:1, :]


def high_low(value):
    high = value.astype(BF16)
    return high, (value - high.astype(F32)).astype(BF16)


def flat(ref):
    return ref[...].reshape(ref.shape[0] * ref.shape[1], ref.shape[2])


def by_core(columns):
    groups, part = CHIP_COUNT, columns.shape[0] // (2 * CHIP_COUNT)
    columns = columns.reshape(groups, 2, part, columns.shape[1])
    return [columns[:, core].reshape(groups * part, columns.shape[3]) for core in range(2)]


def first_kernel(fine_ref, out_ref):
    out_ref[...] = jnp.broadcast_to(fine_ref[...].astype(BF16)[None], out_ref.shape)


def coarse_split_kernel(sizes, coarse_ref, coarse_c_ref, mine_ref, core_ref):
    core = lax.axis_index("c")
    slots = (core, 1 - core)
    own = mine_ref.shape[0]
    block = (lax.axis_index("zl") * sizes["xh"] + lax.axis_index("xh")) * sizes["zh"] + lax.axis_index("zh")
    mine_ref[...] = coarse_ref[pl.ds(pl.multiple_of(block * own, own), own), :]
    core_ref[...] = jnp.full(core_ref.shape, core, jnp.int32)
    for at, columns in enumerate(by_core(coarse_ref[...].astype(BF16).T)):
        coarse_c_ref[slots[at]] = columns.T


def own_scores_kernel(points_ref, own_ref, turned_ref, rest_ref, products_ref, norms_ref):
    core = lax.axis_index("c")
    slots = (core, 1 - core)
    own = flat(own_ref)
    norms_ref[...] = norms_of(own)
    n = products_ref.shape[0]
    tile = min(256, n)
    for start in range(0, n, tile):
        for at, columns in enumerate(by_core(points_ref[start:start + tile, :].T)):
            turned_ref[slots[at], :, start:start + tile] = columns
        rest_ref[start:start + tile, :] = turned_ref[1, :, start:start + tile].T
        products_ref[start:start + tile, :] = jnp.dot(
            turned_ref[0, :, start:start + tile].T, own, preferred_element_type=F32
        )


def norms_of(features):
    total = jnp.zeros((1, features.shape[1]), F32)
    for start in range(0, features.shape[0], LANES):
        total = total + jnp.sum(jnp.square(features[start:start + LANES].astype(F32)), axis=0, keepdims=True)
    return total


def fine_scores_kernel(scale, points_ref, products_ref, norms_ref, other_ref, w_ref, high_ref, lse_ref):
    other = flat(other_ref)
    norms = (norms_ref[...] + norms_of(other)) / scale
    n = products_ref.shape[0]
    tile = min(256, n)
    for start in range(0, n, tile):
        products = products_ref[start:start + tile, :] + jnp.dot(
            points_ref[start:start + tile, :], other, preferred_element_type=F32
        )
        scores = products * (2.0 / scale) - norms
        high = jnp.max(scores, axis=1, keepdims=True)
        weights = jnp.exp2(scores - high)
        w_ref[start:start + tile, :] = weights.astype(BF16)
        lse = to_row(high + jnp.log2(jnp.sum(weights, axis=1, keepdims=True)))
        high_ref[:, start:start + tile] = to_row(high)
        lse_ref[:, :, start:start + tile] = jnp.broadcast_to(lse[None], (lse_ref.shape[0], 1, tile))


def log_sum(ref):
    rows = ref[:, 0, :]
    top = jnp.max(rows, axis=0, keepdims=True)
    return top + jnp.log2(jnp.sum(jnp.exp2(rows - top), axis=0, keepdims=True))


def numer_send_kernel(points_t_ref, w_ref, high_ref, lses_ref, send_ref, factor_ref):
    factor = jnp.exp2(high_ref[...] - log_sum(lses_ref))
    factor_ref[...] = factor
    _, half, n = points_t_ref.shape
    scaled = (points_t_ref[1].astype(F32) * factor).astype(BF16)
    high, low = high_low(factor)
    left = jnp.concatenate([scaled, high, low, jnp.zeros((14, n), BF16)], axis=0)
    sums = jnp.dot(left, w_ref[...], preferred_element_type=F32)
    send_ref[0:half, :] = sums[0:half].astype(BF16)
    high, low = high_low(sums[half:half + 1] + sums[half + 1:half + 2])
    send_ref[half:half + 16, :] = jnp.concatenate([high, low, jnp.zeros((14, high.shape[1]), BF16)], axis=0)


def numer_keep_kernel(points_t_ref, w_ref, factor_ref, keep_ref):
    scaled = (points_t_ref[0].astype(F32) * factor_ref[...]).astype(BF16)
    keep_ref[...] = jnp.dot(scaled, w_ref[...], preferred_element_type=F32)


def pair_kernel(keep_ref, came_ref, sent_ref, out_ref):
    groups = out_ref.shape[0]
    half, k = keep_ref.shape
    part, blocks = half // groups, k // LANES
    numer = (keep_ref[...] + came_ref[0:half, :].astype(F32)).astype(BF16)
    tail = came_ref[half:half + 16, :].astype(F32) + sent_ref[half:half + 16, :].astype(F32)
    counts = tail[0:1] + tail[1:2]
    counts = jnp.concatenate([counts[:, at:at + LANES] for at in range(0, k, LANES)], axis=0)
    counts = jnp.concatenate(high_low(counts), axis=0)
    for group in range(groups):
        for block in range(blocks):
            out_ref[group, block * part:(block + 1) * part, :] = numer[
                group * part:(group + 1) * part, block * LANES:(block + 1) * LANES
            ]
        out_ref[group, blocks * part:blocks * part + 2 * blocks, :] = counts


def new_fine_kernel(came_ref, fine_ref, new_ref, send_ref):
    groups = came_ref.shape[0]
    part, k = new_ref.shape
    blocks = k // LANES
    counts = jnp.sum(came_ref[:, blocks * part:blocks * part + 2 * blocks, :].astype(F32), axis=0)
    counts = counts[0:blocks] + counts[blocks:2 * blocks] + PRIOR
    for block in range(blocks):
        lanes = slice(block * LANES, (block + 1) * LANES)
        numer = jnp.sum(came_ref[:, block * part:(block + 1) * part, :].astype(F32), axis=0)
        new = (numer + fine_ref[:, lanes]) / counts[block:block + 1]
        new_ref[:, lanes] = new
        send_ref[:, :, lanes] = jnp.broadcast_to(new.astype(BF16)[None], (groups, part, LANES))


def own_coarse_kernel(coarse_ref, own_ref, products_ref):
    products_ref[...] = jnp.dot(coarse_ref[0], flat(own_ref), preferred_element_type=F32)


def coarse_scores_kernel(scale, coarse_ref, products_ref, other_ref, w_ref, high_ref, lse_ref):
    norms = jnp.zeros((coarse_ref.shape[1], 1), F32)
    for half in range(2):
        norms = norms + jnp.sum(jnp.square(coarse_ref[half].astype(F32)), axis=1, keepdims=True)
    norms = norms / scale
    products = products_ref[...] + jnp.dot(coarse_ref[1], flat(other_ref), preferred_element_type=F32)
    scores = products * (2.0 / scale) - norms
    high = jnp.max(scores, axis=0, keepdims=True)
    weights = jnp.exp2(scores - high)
    w_ref[...] = weights
    high_ref[...] = high
    lse = high + jnp.log2(jnp.sum(weights, axis=0, keepdims=True))
    lse_ref[...] = jnp.broadcast_to(lse[None], lse_ref.shape)


def tail_of(counts):
    lane = lax.broadcasted_iota(jnp.int32, (counts.shape[0], LANES), 1)
    high = counts.astype(BF16).astype(F32)
    return jnp.where(lane == 0, high, jnp.where(lane == 1, counts - high, 0.0)).astype(BF16)


def coarse_numer_kernel(w_ref, high_ref, lses_ref, own_ref, other_ref, send_ref):
    factor = jnp.exp2(high_ref[...] - log_sum(lses_ref))
    blocks, rows, wide = send_ref.shape
    half_d = (wide - LANES) // 2
    assigned = w_ref[...] * factor
    assigned_b = assigned.astype(BF16)
    for at, ref in enumerate((own_ref, other_ref)):
        numer = lax.dot_general(
            assigned_b, flat(ref), (((1,), (1,)), ((), ())), preferred_element_type=F32
        )
        send_ref[:, :, at * half_d:(at + 1) * half_d] = numer.astype(BF16).reshape(blocks, rows, half_d)
    tail = tail_of(jnp.sum(assigned, axis=1, keepdims=True))
    send_ref[:, :, 2 * half_d:wide] = tail.reshape(blocks, rows, LANES)


def coarse_partial_kernel(came_ref, send_ref):
    far, own, wide = send_ref.shape
    d = wide - LANES
    sums = jnp.sum(came_ref[...].astype(F32), axis=0)
    send_ref[:, :, 0:d] = sums[:, 0:d].astype(BF16).reshape(far, own, d)
    tail = tail_of(sums[:, d:d + 1] + sums[:, d + 1:d + 2])
    send_ref[:, :, d:d + LANES] = tail.reshape(far, own, LANES)


def new_coarse_kernel(core_ref, came_ref, mine_ref, send_ref):
    d = send_ref.shape[2]
    half_d, part = d // 2, d // (2 * CHIP_COUNT)
    sums = jnp.sum(came_ref[...].astype(F32), axis=0)
    counts = sums[:, d:d + 1] + sums[:, d + 1:d + 2]
    first = core_ref[:, 0:1] == 0
    own, other = sums[:, 0:half_d], sums[:, half_d:d]
    by_core = (jnp.where(first, own, other), jnp.where(first, other, own))
    numer = jnp.concatenate(
        [by_core[core][:, at:at + part] for at in range(0, half_d, part) for core in range(2)], axis=1
    )
    new = (numer + mine_ref[...]) / (counts + PRIOR)
    send_ref[...] = jnp.broadcast_to(new.astype(BF16)[None], send_ref.shape)


def repeat_kernel(came_ref, send_ref):
    send_ref[...] = jnp.broadcast_to(flat(came_ref)[None], send_ref.shape)


def widen_kernel(came_ref, out_ref):
    out_ref[...] = flat(came_ref).astype(F32)


def local(sizes, points, fine_centroids, coarse_centroids):
    n, d = points.shape
    k, part = fine_centroids.shape
    rows = coarse_centroids.shape[0]
    groups, near, far = sizes["y"] * sizes["xl"], sizes["zl"] * sizes["xh"], sizes["zh"]
    scale = math.sqrt(d) * math.log(2.0)
    half_d, near_rows, own_rows = d // 2, rows // near, rows // (near * far)
    fine_t = fine_centroids.T

    coarse_c, mine, core = call(
        functools.partial(coarse_split_kernel, sizes),
        (shape_of((2, rows, half_d), BF16), shape_of((own_rows, d), F32), shape_of((own_rows, LANES), jnp.int32)),
        (), (coarse_centroids,),
    )
    own = exchange(call(first_kernel, shape_of((groups, part, k), BF16), (), (fine_t,)), CHIPS)
    other = swap(own, "c")
    turned, rest, products, norms = call(
        own_scores_kernel,
        (shape_of((2, half_d, n), BF16), shape_of((n, half_d), BF16), shape_of((n, k), F32), shape_of((1, k), F32)),
        (), (points, own),
        cost=pl.CostEstimate(flops=8 * n * d * k, bytes_accessed=48 * n * k, transcendentals=0),
    )
    w, high, lses = call(
        functools.partial(fine_scores_kernel, scale),
        (shape_of((n, k), BF16), shape_of((1, n), F32), shape_of((far * near, 1, n), F32)),
        (), (rest, products, norms, other),
    )
    lses = exchange(lses, ("zh",) + NEAR)
    send, factor = call(
        numer_send_kernel, (shape_of((half_d + 16, k), BF16), shape_of((1, n), F32)),
        (), (turned, w, high, lses),
    )
    came = swap(send, "c")
    keep = call(
        numer_keep_kernel, shape_of((half_d, k), F32), (), (turned, w, factor),
        cost=pl.CostEstimate(flops=n * d * k, bytes_accessed=6 * n * k, transcendentals=0),
    )
    tall = (part + 2) * (k // LANES)
    summed = exchange(call(pair_kernel, shape_of((groups, tall, LANES), BF16), (), (keep, came, send)), CHIPS)
    new_fine_t, blocks = call(
        new_fine_kernel, (shape_of((part, k), F32), shape_of((groups, part, k), BF16)), (), (summed, fine_t)
    )
    own = exchange(blocks, CHIPS)
    other = swap(own, "c")
    products = call(
        own_coarse_kernel, shape_of((rows, k), F32), (), (coarse_c, own),
        cost=pl.CostEstimate(flops=rows * d * k, bytes_accessed=6 * rows * k, transcendentals=0),
    )
    w, high, lses = call(
        functools.partial(coarse_scores_kernel, scale),
        (shape_of((rows, k), F32), shape_of((1, k), F32), shape_of((groups * 2, 1, k), F32)),
        (), (coarse_c, products, other),
    )
    lses = exchange(lses, CHIPS + ("c",))
    wide = d + LANES
    summed = call(coarse_numer_kernel, shape_of((near, near_rows, wide), BF16), (), (w, high, lses, own, other))
    summed = exchange(summed, NEAR)
    summed = exchange(call(coarse_partial_kernel, shape_of((far, own_rows, wide), BF16), (), (summed,)), "zh")
    blocks = call(new_coarse_kernel, shape_of((far, own_rows, d), BF16), (), (core, summed, mine))
    blocks = call(repeat_kernel, shape_of((near, near_rows, d), BF16), (), (exchange(blocks, "zh"),))
    new_coarse = call(widen_kernel, shape_of((rows, d), F32), (), (exchange(blocks, NEAR),))
    return (new_fine_t.T, new_coarse)


def solution(mesh):
    sizes = {"y": 4, "xl": 2, "c": 2, "zh": 8, "zl": 2, "xh": 2}
    fine_mesh = Mesh(mesh.devices.reshape(tuple(sizes.values())), tuple(sizes))
    dp, mp = ("y", "xl", "c"), ("zh", "zl", "xh")
    in_specs = (P(dp, None), P(mp, dp), P(dp, None))
    out_specs = (P(mp, dp), P(dp, None))
    run = functools.partial(local, sizes)
    return jax.shard_map(run, mesh=fine_mesh, in_specs=in_specs, out_specs=out_specs, check_vma=False)
```

time: 773 us -> 186 us (0.24)
  waiting for transfers between devices: 398 us -> 3.85 us
  blocking collectives: 302 us -> 163 us
  other arithmetic: 19.9 us -> 0 us
  matrix products: 19.7 us -> 0 us
  between operations: 13.8 us -> 0.75 us
  Pallas kernels: 0 us -> 11.5 us
    psum x1 -> x0, waiting for transfers between devices: 236 us -> none  [local(): coarse_numer, coarse_counts = lax.psum((coarse_numer, coarse_counts), 'mp')]
    psum x4 -> x0, blocking collectives: 200 us -> none  [the longest x1 78.2 us: local(): coarse_numer, coarse_counts = lax.psum((coarse_numer, coarse_counts), 'mp')]
    all_to_all x0 -> x9, blocking collectives: none -> 163 us  [exchange(): return lax.all_to_all(blocks, axis, split_axis=0, concat_axis=0, tiled=True)]
    pmax x2 -> x0, blocking collectives: 102 us -> none  [the longest x1 78.1 us: local(): highest = lax.pmax(jnp.max(scores, axis=1), 'mp')]
    all_gather x2 -> x0, waiting for transfers between devices: 93.7 us -> none  [the longest x1 47.4 us: local(): shard_cols = lax.all_gather(fine_b, 'dp', axis=1, tiled=True)]
    reduce_scatter x1 -> x0, waiting for transfers between devices: 68.4 us -> none  [local(): lax.psum_scatter(contract_points(assigned_b, points), 'dp', scatter_dimen...]
    dot_general x4 -> x0, matrix products: 19.7 us -> none  [the longest x2 10.4 us: contract_points(): lax.dot_general(weights_b, values_b, (((0,), (0,)), ((), ())), preferred_...]
    reduce_sum x6 -> x0, other arithmetic: 11.8 us -> none  [the longest x1 3.52 us: local(): fine_counts = jnp.sum(assigned, axis=0)]
  transfers between devices with their start and end apart: 5 -> 3, of which waited for: 4 -> 3; matrix products, arithmetic and copies ran while one was open for 1% -> 0% of each run, Pallas kernels for 0% -> 2%
where the time goes in v1:
time: 186 us
  blocking collectives  163 us (88%)
  Pallas kernels  11.5 us (6%)
  starting transfers between devices  5.74 us (3%)
  waiting for transfers between devices  3.85 us (2%)
    all_to_all x9, blocking collectives, exchange(): return lax.all_to_all(blocks, axis, split_axis=0, concat_axis=0, tiled=True)  163 us
    pallas_call x15, Pallas kernels, call(): pl.pallas_call(kernel, out_shape=out_shape, in_specs=specs, out_specs=out...  11.5 us
    ppermute x3, starting transfers between devices, swap(): return lax.ppermute(block, axis, PAIR)  5.74 us
    ppermute x3, waiting for transfers between devices, swap(): return lax.ppermute(block, axis, PAIR)  3.85 us
  transfers between devices with their start and end apart: 3, of which 3 were waited for; matrix products, arithmetic and copies ran while one was open for 0% of the time, Pallas kernels for 2%

profile of v1, /device:TPU:8, one launch (start us, length us, event | category | flops | bytes accessed | tf_op | source)
XLA Modules:
  0.0 185.7 jit_solution(6219783936464009519)
XLA Ops:
  0.6 0.0 copy-start.1
  0.6 0.9 copy-done.1
  1.6 0.0 copy-start.3
  1.6 0.1 shard_map.50
  1.7 19.7 %all_to_all.45.own_ref = bf16[8,64,1024]{2,1,0:T(8,128)(2,1)S(1)} all-to-all(bf16[8,64,1024]{2,1,0:T(8,128)(2,1)S(1)} %shard_map.50), channel_id=1, replica_groups=mesh['y'=4,'xl'=2,'c'=2,'zh'=8,'zl'=2,'xh'=2] {'y','xl'}, dimensions={0} | all-to-all | bytes 2097152 | tf_op jit(solution)/shard_map/all_to_all | solution.py:41
  21.4 1.9 %collective-permute-start = (bf16[8,64,1024]{2,1,0:T(8,128)(2,1)S(1)}, bf16[8,64,1024]{2,1,0:T(8,128)(2,1)S(1)}, u32[]{:S(2)}, u32[]{:S(2)}) collective-permute-start(bf16[8,64,1024]{2,1,0:T(8,128)(2,1)S(1)} %all_to_all.45.own_ref), channel_id=1, source_target_pairs={{0,32},{32,0},{1,33},{33,1},{2,34},{34,2},{3,35},{35,3},{4,36},{36... | collective-permute-start | bytes 3145736 | tf_op jit(solution)/shard_map/ppermute | solution.py:45
  23.3 0.0 copy-done.3
  23.3 2.0 %shard_map.51 = (bf16[2,512,1024]{2,1,0:T(8,128)(2,1)S(1)}, bf16[1024,512]{1,0:T(8,128)(2,1)S(1)}, f32[1024,1024]{1,0:T(8,128)S(1)}, f32[1,1024]{1,0:T(1,128)S(1)}) custom-call(bf16[1024,1024]{1,0:T(8,128)(2,1)S(1)} %copy-done.3, bf16[8,64,1024]{2,1,0:T(8,128)(2,1)S(1)} %all_to_all.45.own_ref), custom_call_target="tpu_custom_call" | custom-call | flops 8589934592 | bytes 50331648 | tf_op jit(solution)/shard_map/pallas_call | solution.py:30
  25.3 0.6 collective-permute-done.other_ref
  25.9 2.1 %shard_map.52 = (bf16[1024,1024]{1,0:T(8,128)(2,1)S(1)}, f32[1,1024]{1,0:T(1,128)S(1)}, f32[32,1,1024]{2,1,0:T(1,128)S(1)}) custom-call(bf16[1024,512]{1,0:T(8,128)(2,1)S(1)} %get-tuple-element.20.points_ref, f32[1024,1024]{1,0:T(8,128)S(1)} %get-tuple-element.21.products_ref, f32[1,1024]{1,0:T(1,128)S(1)} %get-tuple-element.22.norms_ref, ...), custom_call_target="tpu_custom_call" | custom-call | tf_op jit(solution)/shard_map/pallas_call | solution.py:30
  28.0 35.1 %all_to_all.46.lses_ref = f32[32,1,1024]{2,1,0:T(1,128)S(1)} all-to-all(f32[32,1,1024]{2,1,0:T(1,128)S(1)} %get-tuple-element.25), channel_id=1, replica_groups=mesh['y'=4,'xl'=2,'c'=2,'zh'=8,'zl'=2,'xh'=2] {'zh','zl','xh'}, dimensions={0} | all-to-all | bytes 262144 | tf_op jit(solution)/shard_map/all_to_all | solution.py:41
  63.2 1.4 shard_map.53
  64.5 1.9 %collective-permute-start.1 = (bf16[528,1024]{1,0:T(8,128)(2,1)S(1)}, bf16[528,1024]{1,0:T(8,128)(2,1)S(1)}, u32[]{:S(2)}, u32[]{:S(2)}) collective-permute-start(bf16[528,1024]{1,0:T(8,128)(2,1)S(1)} %get-tuple-element.27.sent_ref), channel_id=1, source_target_pairs={{0,32},{32,0},{1,33},{33,1},{2,34},{34,2},{3,35},{35,3},{4,36},{36... | collective-permute-start | bytes 3244040 | tf_op jit(solution)/shard_map/ppermute | solution.py:45
  66.4 1.3 shard_map.54.keep_ref
  67.7 1.4 collective-permute-done.1.came_ref
  69.1 0.2 shard_map.55
  69.3 0.0 copy-start.2
  69.3 19.8 %all_to_all.47.came_ref = bf16[8,528,128]{2,1,0:T(8,128)(2,1)S(1)} all-to-all(bf16[8,528,128]{2,1,0:T(8,128)(2,1)S(1)} %shard_map.55), channel_id=1, replica_groups=mesh['y'=4,'xl'=2,'c'=2,'zh'=8,'zl'=2,'xh'=2] {'y','xl'}, dimensions={0} | all-to-all | bytes 2162688 | tf_op jit(solution)/shard_map/all_to_all | solution.py:41
  89.1 0.0 copy-done.2
  89.1 0.0 copy-start
  89.1 1.0 shard_map.56
  90.1 17.6 %all_to_all.48.own_ref = bf16[8,64,1024]{2,1,0:T(8,128)(2,1)S(1)} all-to-all(bf16[8,64,1024]{2,1,0:T(8,128)(2,1)S(1)} %get-tuple-element.31), channel_id=1, replica_groups=mesh['y'=4,'xl'=2,'c'=2,'zh'=8,'zl'=2,'xh'=2] {'y','xl'}, dimensions={0} | all-to-all | bytes 2097152 | tf_op jit(solution)/shard_map/all_to_all | solution.py:41
  107.7 1.9 %collective-permute-start.2 = (bf16[8,64,1024]{2,1,0:T(8,128)(2,1)S(1)}, bf16[8,64,1024]{2,1,0:T(8,128)(2,1)S(1)}, u32[]{:S(2)}, u32[]{:S(2)}) collective-permute-start(bf16[8,64,1024]{2,1,0:T(8,128)(2,1)S(1)} %all_to_all.48.own_ref), channel_id=1, source_target_pairs={{0,32},{32,0},{1,33},{33,1},{2,34},{34,2},{3,35},{35,3},{4,36},{36... | collective-permute-start | bytes 3145736 | tf_op jit(solution)/shard_map/ppermute | solution.py:45
  109.6 0.0 copy-done
  109.6 0.3 shard_map.57
  109.9 0.4 shard_map.58.products_ref
  110.4 1.8 collective-permute-done.2.other_ref
  112.2 0.6 shard_map.59
  112.8 9.1 %all_to_all.49.lses_ref = f32[16,1,1024]{2,1,0:T(1,128)S(1)} all-to-all(f32[16,1,1024]{2,1,0:T(1,128)S(1)} %get-tuple-element.34), channel_id=1, replica_groups=mesh['y'=4,'xl'=2,'c'=2,'zh'=8,'zl'=2,'xh'=2] {'y','xl','c'}, dimensions={0} | all-to-all | bytes 131072 | tf_op jit(solution)/shard_map/all_to_all | solution.py:41
  121.9 0.7 shard_map.60
  122.6 14.2 %all_to_all.50.came_ref = bf16[4,64,1152]{2,1,0:T(8,128)(2,1)S(1)} all-to-all(bf16[4,64,1152]{2,1,0:T(8,128)(2,1)S(1)} %shard_map.60), channel_id=1, replica_groups=mesh['y'=4,'xl'=2,'c'=2,'zh'=8,'zl'=2,'xh'=2] {'zl','xh'}, dimensions={0} | all-to-all | bytes 1179648 | tf_op jit(solution)/shard_map/all_to_all | solution.py:41
  136.8 0.2 shard_map.61
  137.0 18.9 %all_to_all.51.came_ref = bf16[8,8,1152]{2,1,0:T(8,128)(2,1)S(1)} all-to-all(bf16[8,8,1152]{2,1,0:T(8,128)(2,1)S(1)} %shard_map.61), channel_id=1, replica_groups=mesh['y'=4,'xl'=2,'c'=2,'zh'=8,'zl'=2,'xh'=2] {'zh'}, dimensions={0} | all-to-all | bytes 294912 | tf_op jit(solution)/shard_map/all_to_all | solution.py:41
  155.8 0.2 shard_map.62
  156.0 17.5 %all_to_all.52.came_ref = bf16[8,8,1024]{2,1,0:T(8,128)(2,1)S(1)} all-to-all(bf16[8,8,1024]{2,1,0:T(8,128)(2,1)S(1)} %shard_map.62), channel_id=1, replica_groups=mesh['y'=4,'xl'=2,'c'=2,'zh'=8,'zl'=2,'xh'=2] {'zh'}, dimensions={0} | all-to-all | bytes 262144 | tf_op jit(solution)/shard_map/all_to_all | solution.py:41
  173.6 11.0 %all_to_all.53.came_ref = bf16[4,64,1024]{2,1,0:T(8,128)(2,1)S(1)} all-to-all(bf16[4,64,1024]{2,1,0:T(8,128)(2,1)S(1)} %shard_map.63), channel_id=1, replica_groups=mesh['y'=4,'xl'=2,'c'=2,'zh'=8,'zl'=2,'xh'=2] {'zl','xh'}, dimensions={0} | all-to-all | bytes 1048576 | tf_op jit(solution)/shard_map/all_to_all | solution.py:41
  184.6 1.0 shard_map.64
  (1 shorter events, 0.0 us)
Async XLA Ops:
  0.6 1.0 copy-start.1
  1.6 21.7 %copy-start.3 = (bf16[1024,1024]{1,0:T(8,128)(2,1)S(1)}, bf16[1024,1024]{1,0:T(8,128)(2,1)}, u32[]{:S(2)}) copy-start(bf16[1024,1024]{1,0:T(8,128)(2,1)} %points_ref.1) | copy-start | bytes 6291460
  21.4 4.5 %collective-permute-start = (bf16[8,64,1024]{2,1,0:T(8,128)(2,1)S(1)}, bf16[8,64,1024]{2,1,0:T(8,128)(2,1)S(1)}, u32[]{:S(2)}, u32[]{:S(2)}) collective-permute-start(bf16[8,64,1024]{2,1,0:T(8,128)(2,1)S(1)} %all_to_all.45.own_ref), channel_id=1, source_target_pairs={{0,32},{32,0},{1,33},{33,1},{2,34},{34,2},{3,35},{35,3},{4,36},{36... | collective-permute-start | bytes 3145736 | tf_op jit(solution)/shard_map/ppermute | solution.py:45
  64.5 4.6 %collective-permute-start.1 = (bf16[528,1024]{1,0:T(8,128)(2,1)S(1)}, bf16[528,1024]{1,0:T(8,128)(2,1)S(1)}, u32[]{:S(2)}, u32[]{:S(2)}) collective-permute-start(bf16[528,1024]{1,0:T(8,128)(2,1)S(1)} %get-tuple-element.27.sent_ref), channel_id=1, source_target_pairs={{0,32},{32,0},{1,33},{33,1},{2,34},{34,2},{3,35},{35,3},{4,36},{36... | collective-permute-start | bytes 3244040 | tf_op jit(solution)/shard_map/ppermute | solution.py:45
  69.3 19.8 %copy-start.2 = (f32[1024,64]{0,1:T(8,128)S(1)}, f32[1024,64]{0,1:T(8,128)}, u32[]{:S(2)}) copy-start(f32[1024,64]{0,1:T(8,128)} %param.4) | copy-start | bytes 786436
  89.1 20.5 %copy-start = (f32[256,1024]{1,0:T(8,128)S(1)}, f32[256,1024]{1,0:T(8,128)}, u32[]{:S(2)}) copy-start(f32[256,1024]{1,0:T(8,128)} %coarse_ref.1) | copy-start | bytes 3145732
  107.7 4.5 %collective-permute-start.2 = (bf16[8,64,1024]{2,1,0:T(8,128)(2,1)S(1)}, bf16[8,64,1024]{2,1,0:T(8,128)(2,1)S(1)}, u32[]{:S(2)}, u32[]{:S(2)}) collective-permute-start(bf16[8,64,1024]{2,1,0:T(8,128)(2,1)S(1)} %all_to_all.48.own_ref), channel_id=1, source_target_pairs={{0,32},{32,0},{1,33},{33,1},{2,34},{34,2},{3,35},{35,3},{4,36},{36... | collective-permute-start | bytes 3145736 | tf_op jit(solution)/shard_map/ppermute | solution.py:45

commit v2 on v1

--- a/solution.py
+++ b/solution.py
@@ -12,9 +12,11 @@
 F32, BF16 = jnp.float32, jnp.bfloat16
 LANES = 128
 PAIR = [(0, 1), (1, 0)]
-CHIPS = ("y", "xl")
-NEAR = ("zl", "xh")
+CHIPS = ("xl", "y")
+NEAR = ("xh", "zl")
 CHIP_COUNT = 8
+ORDER = (0, 2, 4, 6, 1, 3, 5, 7)
+ORDER_BACK = (0, 4, 1, 5, 2, 6, 3, 7)
 VMEM = pl.BlockSpec(memory_space=pltpu.VMEM)
 SMEM = pl.BlockSpec(memory_space=pltpu.SMEM)
 PARAMS = pltpu.CompilerParams(vmem_limit_bytes=24 * 1024 * 1024)
@@ -59,9 +61,9 @@
 
 
 def by_core(columns):
-    groups, part = CHIP_COUNT, columns.shape[0] // (2 * CHIP_COUNT)
-    columns = columns.reshape(groups, 2, part, columns.shape[1])
-    return [columns[:, core].reshape(groups * part, columns.shape[3]) for core in range(2)]
+    part = columns.shape[0] // (2 * CHIP_COUNT)
+    parts = [columns[at:at + part] for at in range(0, columns.shape[0], part)]
+    return [jnp.concatenate([parts[2 * chip + core] for chip in ORDER], axis=0) for core in range(2)]
 
 
 def first_kernel(fine_ref, out_ref):
@@ -72,7 +74,7 @@
     core = lax.axis_index("c")
     slots = (core, 1 - core)
     own = mine_ref.shape[0]
-    block = (lax.axis_index("zl") * sizes["xh"] + lax.axis_index("xh")) * sizes["zh"] + lax.axis_index("zh")
+    block = (lax.axis_index("xh") * sizes["zl"] + lax.axis_index("zl")) * sizes["zh"] + lax.axis_index("zh")
     mine_ref[...] = coarse_ref[pl.ds(pl.multiple_of(block * own, own), own), :]
     core_ref[...] = jnp.full(core_ref.shape, core, jnp.int32)
     for at, columns in enumerate(by_core(coarse_ref[...].astype(BF16).T)):
@@ -233,7 +235,7 @@
     own, other = sums[:, 0:half_d], sums[:, half_d:d]
     by_core = (jnp.where(first, own, other), jnp.where(first, other, own))
     numer = jnp.concatenate(
-        [by_core[core][:, at:at + part] for at in range(0, half_d, part) for core in range(2)], axis=1
+        [by_core[core][:, at * part:(at + 1) * part] for at in ORDER_BACK for core in range(2)], axis=1
     )
     new = (numer + mine_ref[...]) / (counts + PRIOR)
     send_ref[...] = jnp.broadcast_to(new.astype(BF16)[None], send_ref.shape)
@@ -274,7 +276,7 @@
         (shape_of((n, k), BF16), shape_of((1, n), F32), shape_of((far * near, 1, n), F32)),
         (), (rest, products, norms, other),
     )
-    lses = exchange(lses, ("zh",) + NEAR)
+    lses = exchange(lses, NEAR + ("zh",))
     send, factor = call(
         numer_send_kernel, (shape_of((half_d + 16, k), BF16), shape_of((1, n), F32)),
         (), (turned, w, high, lses),
@@ -300,7 +302,7 @@
         (shape_of((rows, k), F32), shape_of((1, k), F32), shape_of((groups * 2, 1, k), F32)),
         (), (coarse_c, products, other),
     )
-    lses = exchange(lses, CHIPS + ("c",))
+    lses = exchange(lses, ("c",) + CHIPS)
     wide = d + LANES
     summed = call(coarse_numer_kernel, shape_of((near, near_rows, wide), BF16), (), (w, high, lses, own, other))
     summed = exchange(summed, NEAR)

time: 186 us -> 185 us (level)
  the two profiles are of different devices: /device:TPU:8 before, /device:TPU:32 now
where the time goes in v2:
time: 185 us
  blocking collectives  162 us (88%)
  Pallas kernels  11.5 us (6%)
  starting transfers between devices  5.74 us (3%)
  waiting for transfers between devices  3.93 us (2%)
    all_to_all x9, blocking collectives, exchange(): return lax.all_to_all(blocks, axis, split_axis=0, concat_axis=0, tiled=True)  162 us
    pallas_call x15, Pallas kernels, call(): pl.pallas_call(kernel, out_shape=out_shape, in_specs=specs, out_specs=out...  11.5 us
    ppermute x3, starting transfers between devices, swap(): return lax.ppermute(block, axis, PAIR)  5.74 us
    ppermute x3, waiting for transfers between devices, swap(): return lax.ppermute(block, axis, PAIR)  3.93 us
  transfers between devices with their start and end apart: 3, of which 3 were waited for; matrix products, arithmetic and copies ran while one was open for 0% of the time, Pallas kernels for 2%

profile of v2, /device:TPU:32, one launch (start us, length us, event | category | flops | bytes accessed | tf_op | source)
XLA Modules:
  0.0 184.9 jit_solution(3904606851906068172)
XLA Ops:
  0.6 0.0 copy-start.1
  0.6 0.9 copy-done.1
  1.6 0.0 copy-start.3
  1.6 0.1 shard_map.50
  1.7 21.1 %all_to_all.45.own_ref = bf16[8,64,1024]{2,1,0:T(8,128)(2,1)S(1)} all-to-all(bf16[8,64,1024]{2,1,0:T(8,128)(2,1)S(1)} %shard_map.50), channel_id=1, replica_groups=mesh['y'=4,'xl'=2,'c'=2,'zh'=8,'zl'=2,'xh'=2] {'xl','y'}, dimensions={0} | all-to-all | bytes 2097152 | tf_op jit(solution)/shard_map/all_to_all | solution.py:43
  22.8 1.9 %collective-permute-start = (bf16[8,64,1024]{2,1,0:T(8,128)(2,1)S(1)}, bf16[8,64,1024]{2,1,0:T(8,128)(2,1)S(1)}, u32[]{:S(2)}, u32[]{:S(2)}) collective-permute-start(bf16[8,64,1024]{2,1,0:T(8,128)(2,1)S(1)} %all_to_all.45.own_ref), channel_id=1, source_target_pairs={{0,32},{32,0},{1,33},{33,1},{2,34},{34,2},{3,35},{35,3},{4,36},{36... | collective-permute-start | bytes 3145736 | tf_op jit(solution)/shard_map/ppermute | solution.py:47
  24.7 0.0 copy-done.3
  24.7 1.9 %shard_map.51 = (bf16[2,512,1024]{2,1,0:T(8,128)(2,1)S(1)}, bf16[1024,512]{1,0:T(8,128)(2,1)S(1)}, f32[1024,1024]{1,0:T(8,128)S(1)}, f32[1,1024]{1,0:T(1,128)S(1)}) custom-call(bf16[1024,1024]{1,0:T(8,128)(2,1)S(1)} %copy-done.3, bf16[8,64,1024]{2,1,0:T(8,128)(2,1)S(1)} %all_to_all.45.own_ref), custom_call_target="tpu_custom_call" | custom-call | flops 8589934592 | bytes 50331648 | tf_op jit(solution)/shard_map/pallas_call | solution.py:32
  26.6 0.7 collective-permute-done.other_ref
  27.3 2.1 %shard_map.52 = (bf16[1024,1024]{1,0:T(8,128)(2,1)S(1)}, f32[1,1024]{1,0:T(1,128)S(1)}, f32[32,1,1024]{2,1,0:T(1,128)S(1)}) custom-call(bf16[1024,512]{1,0:T(8,128)(2,1)S(1)} %get-tuple-element.20.points_ref, f32[1024,1024]{1,0:T(8,128)S(1)} %get-tuple-element.21.products_ref, f32[1,1024]{1,0:T(1,128)S(1)} %get-tuple-element.22.norms_ref, ...), custom_call_target="tpu_custom_call" | custom-call | tf_op jit(solution)/shard_map/pallas_call | solution.py:32
  29.4 33.7 %all_to_all.46.lses_ref = f32[32,1,1024]{2,1,0:T(1,128)S(1)} all-to-all(f32[32,1,1024]{2,1,0:T(1,128)S(1)} %get-tuple-element.25), channel_id=1, replica_groups=mesh['y'=4,'xl'=2,'c'=2,'zh'=8,'zl'=2,'xh'=2] {'xh','zl','zh'}, dimensions={0} | all-to-all | bytes 262144 | tf_op jit(solution)/shard_map/all_to_all | solution.py:43
  63.2 1.4 shard_map.53
  64.5 1.9 %collective-permute-start.1 = (bf16[528,1024]{1,0:T(8,128)(2,1)S(1)}, bf16[528,1024]{1,0:T(8,128)(2,1)S(1)}, u32[]{:S(2)}, u32[]{:S(2)}) collective-permute-start(bf16[528,1024]{1,0:T(8,128)(2,1)S(1)} %get-tuple-element.27.sent_ref), channel_id=1, source_target_pairs={{0,32},{32,0},{1,33},{33,1},{2,34},{34,2},{3,35},{35,3},{4,36},{36... | collective-permute-start | bytes 3244040 | tf_op jit(solution)/shard_map/ppermute | solution.py:47
  66.4 1.3 shard_map.54.keep_ref
  67.7 1.4 collective-permute-done.1.came_ref
  69.1 0.2 shard_map.55
  69.3 0.0 copy-start.2
  69.3 19.4 %all_to_all.47.came_ref = bf16[8,528,128]{2,1,0:T(8,128)(2,1)S(1)} all-to-all(bf16[8,528,128]{2,1,0:T(8,128)(2,1)S(1)} %shard_map.55), channel_id=1, replica_groups=mesh['y'=4,'xl'=2,'c'=2,'zh'=8,'zl'=2,'xh'=2] {'xl','y'}, dimensions={0} | all-to-all | bytes 2162688 | tf_op jit(solution)/shard_map/all_to_all | solution.py:43
  88.7 0.0 copy-done.2
  88.7 0.0 copy-start
  88.7 1.0 shard_map.56
  89.7 18.1 %all_to_all.48.own_ref = bf16[8,64,1024]{2,1,0:T(8,128)(2,1)S(1)} all-to-all(bf16[8,64,1024]{2,1,0:T(8,128)(2,1)S(1)} %get-tuple-element.31), channel_id=1, replica_groups=mesh['y'=4,'xl'=2,'c'=2,'zh'=8,'zl'=2,'xh'=2] {'xl','y'}, dimensions={0} | all-to-all | bytes 2097152 | tf_op jit(solution)/shard_map/all_to_all | solution.py:43
  107.8 1.9 %collective-permute-start.2 = (bf16[8,64,1024]{2,1,0:T(8,128)(2,1)S(1)}, bf16[8,64,1024]{2,1,0:T(8,128)(2,1)S(1)}, u32[]{:S(2)}, u32[]{:S(2)}) collective-permute-start(bf16[8,64,1024]{2,1,0:T(8,128)(2,1)S(1)} %all_to_all.48.own_ref), channel_id=1, source_target_pairs={{0,32},{32,0},{1,33},{33,1},{2,34},{34,2},{3,35},{35,3},{4,36},{36... | collective-permute-start | bytes 3145736 | tf_op jit(solution)/shard_map/ppermute | solution.py:47
  109.7 0.0 copy-done
  109.8 0.3 shard_map.57
  110.1 0.4 shard_map.58.products_ref
  110.5 1.8 collective-permute-done.2.other_ref
  112.4 0.6 shard_map.59
  113.0 8.7 %all_to_all.49.lses_ref = f32[16,1,1024]{2,1,0:T(1,128)S(1)} all-to-all(f32[16,1,1024]{2,1,0:T(1,128)S(1)} %get-tuple-element.34), channel_id=1, replica_groups=mesh['y'=4,'xl'=2,'c'=2,'zh'=8,'zl'=2,'xh'=2] {'c','xl','y'}, dimensions={0} | all-to-all | bytes 131072 | tf_op jit(solution)/shard_map/all_to_all | solution.py:43
  121.7 0.7 shard_map.60
  122.5 13.6 %all_to_all.50.came_ref = bf16[4,64,1152]{2,1,0:T(8,128)(2,1)S(1)} all-to-all(bf16[4,64,1152]{2,1,0:T(8,128)(2,1)S(1)} %shard_map.60), channel_id=1, replica_groups=mesh['y'=4,'xl'=2,'c'=2,'zh'=8,'zl'=2,'xh'=2] {'xh','zl'}, dimensions={0} | all-to-all | bytes 1179648 | tf_op jit(solution)/shard_map/all_to_all | solution.py:43
  136.1 0.2 shard_map.61
  136.2 18.3 %all_to_all.51.came_ref = bf16[8,8,1152]{2,1,0:T(8,128)(2,1)S(1)} all-to-all(bf16[8,8,1152]{2,1,0:T(8,128)(2,1)S(1)} %shard_map.61), channel_id=1, replica_groups=mesh['y'=4,'xl'=2,'c'=2,'zh'=8,'zl'=2,'xh'=2] {'zh'}, dimensions={0} | all-to-all | bytes 294912 | tf_op jit(solution)/shard_map/all_to_all | solution.py:43
  154.6 0.2 shard_map.62
  154.7 17.8 %all_to_all.52.came_ref = bf16[8,8,1024]{2,1,0:T(8,128)(2,1)S(1)} all-to-all(bf16[8,8,1024]{2,1,0:T(8,128)(2,1)S(1)} %shard_map.62), channel_id=1, replica_groups=mesh['y'=4,'xl'=2,'c'=2,'zh'=8,'zl'=2,'xh'=2] {'zh'}, dimensions={0} | all-to-all | bytes 262144 | tf_op jit(solution)/shard_map/all_to_all | solution.py:43
  172.6 11.3 %all_to_all.53.came_ref = bf16[4,64,1024]{2,1,0:T(8,128)(2,1)S(1)} all-to-all(bf16[4,64,1024]{2,1,0:T(8,128)(2,1)S(1)} %shard_map.63), channel_id=1, replica_groups=mesh['y'=4,'xl'=2,'c'=2,'zh'=8,'zl'=2,'xh'=2] {'xh','zl'}, dimensions={0} | all-to-all | bytes 1048576 | tf_op jit(solution)/shard_map/all_to_all | solution.py:43
  183.8 1.0 shard_map.64
  (1 shorter events, 0.0 us)
Async XLA Ops:
  0.6 1.0 copy-start.1
  1.6 23.1 %copy-start.3 = (bf16[1024,1024]{1,0:T(8,128)(2,1)S(1)}, bf16[1024,1024]{1,0:T(8,128)(2,1)}, u32[]{:S(2)}) copy-start(bf16[1024,1024]{1,0:T(8,128)(2,1)} %points_ref.1) | copy-start | bytes 6291460
  22.8 4.5 %collective-permute-start = (bf16[8,64,1024]{2,1,0:T(8,128)(2,1)S(1)}, bf16[8,64,1024]{2,1,0:T(8,128)(2,1)S(1)}, u32[]{:S(2)}, u32[]{:S(2)}) collective-permute-start(bf16[8,64,1024]{2,1,0:T(8,128)(2,1)S(1)} %all_to_all.45.own_ref), channel_id=1, source_target_pairs={{0,32},{32,0},{1,33},{33,1},{2,34},{34,2},{3,35},{35,3},{4,36},{36... | collective-permute-start | bytes 3145736 | tf_op jit(solution)/shard_map/ppermute | solution.py:47
  64.5 4.6 %collective-permute-start.1 = (bf16[528,1024]{1,0:T(8,128)(2,1)S(1)}, bf16[528,1024]{1,0:T(8,128)(2,1)S(1)}, u32[]{:S(2)}, u32[]{:S(2)}) collective-permute-start(bf16[528,1024]{1,0:T(8,128)(2,1)S(1)} %get-tuple-element.27.sent_ref), channel_id=1, source_target_pairs={{0,32},{32,0},{1,33},{33,1},{2,34},{34,2},{3,35},{35,3},{4,36},{36... | collective-permute-start | bytes 3244040 | tf_op jit(solution)/shard_map/ppermute | solution.py:47
  69.3 19.4 %copy-start.2 = (f32[1024,64]{0,1:T(8,128)S(1)}, f32[1024,64]{0,1:T(8,128)}, u32[]{:S(2)}) copy-start(f32[1024,64]{0,1:T(8,128)} %param.4) | copy-start | bytes 786436
  88.7 21.1 %copy-start = (f32[256,1024]{1,0:T(8,128)S(1)}, f32[256,1024]{1,0:T(8,128)}, u32[]{:S(2)}) copy-start(f32[256,1024]{1,0:T(8,128)} %coarse_ref.1) | copy-start | bytes 3145732
  107.8 4.5 %collective-permute-start.2 = (bf16[8,64,1024]{2,1,0:T(8,128)(2,1)S(1)}, bf16[8,64,1024]{2,1,0:T(8,128)(2,1)S(1)}, u32[]{:S(2)}, u32[]{:S(2)}) collective-permute-start(bf16[8,64,1024]{2,1,0:T(8,128)(2,1)S(1)} %all_to_all.48.own_ref), channel_id=1, source_target_pairs={{0,32},{32,0},{1,33},{33,1},{2,34},{34,2},{3,35},{35,3},{4,36},{36... | collective-permute-start | bytes 3145736 | tf_op jit(solution)/shard_map/ppermute | solution.py:47

commit v3 on v2

--- a/solution.py
+++ b/solution.py
@@ -70,13 +70,14 @@
     out_ref[...] = jnp.broadcast_to(fine_ref[...].astype(BF16)[None], out_ref.shape)
 
 
-def coarse_split_kernel(sizes, coarse_ref, coarse_c_ref, mine_ref, core_ref):
+def coarse_split_kernel(sizes, coarse_ref, new_ref, coarse_c_ref, mine_ref, core_ref, new_fine_ref):
     core = lax.axis_index("c")
     slots = (core, 1 - core)
     own = mine_ref.shape[0]
     block = (lax.axis_index("xh") * sizes["zl"] + lax.axis_index("zl")) * sizes["zh"] + lax.axis_index("zh")
     mine_ref[...] = coarse_ref[pl.ds(pl.multiple_of(block * own, own), own), :]
     core_ref[...] = jnp.full(core_ref.shape, core, jnp.int32)
+    new_fine_ref[...] = new_ref[...]
     for at, columns in enumerate(by_core(coarse_ref[...].astype(BF16).T)):
         coarse_c_ref[slots[at]] = columns.T
 
@@ -204,26 +205,37 @@
 
 def coarse_numer_kernel(w_ref, high_ref, lses_ref, own_ref, other_ref, send_ref):
     factor = jnp.exp2(high_ref[...] - log_sum(lses_ref))
-    blocks, rows, wide = send_ref.shape
-    half_d = (wide - LANES) // 2
     assigned = w_ref[...] * factor
     assigned_b = assigned.astype(BF16)
-    for at, ref in enumerate((own_ref, other_ref)):
+    near, tall, _ = send_ref.shape
+    rows = assigned.shape[0] // near
+    lane_blocks = (tall - 16) // rows
+    for half, ref in enumerate((own_ref, other_ref)):
         numer = lax.dot_general(
             assigned_b, flat(ref), (((1,), (1,)), ((), ())), preferred_element_type=F32
-        )
-        send_ref[:, :, at * half_d:(at + 1) * half_d] = numer.astype(BF16).reshape(blocks, rows, half_d)
-    tail = tail_of(jnp.sum(assigned, axis=1, keepdims=True))
-    send_ref[:, :, 2 * half_d:wide] = tail.reshape(blocks, rows, LANES)
+        ).astype(BF16).reshape(near, rows, lane_blocks // 2 * LANES)
+        for block in range(lane_blocks // 2):
+            at = (half * (lane_blocks // 2) + block) * rows
+            send_ref[:, at:at + rows, :] = numer[:, :, block * LANES:(block + 1) * LANES]
+    counts = to_row(jnp.sum(assigned, axis=1, keepdims=True))
+    counts = jnp.concatenate([counts[:, at:at + LANES] for at in range(0, counts.shape[1], LANES)], axis=0)
+    high = counts.astype(BF16).astype(F32)
+    pad = jnp.zeros((16 - 2 * counts.shape[0], LANES), F32)
+    tail = jnp.concatenate([high, counts - high, pad], axis=0).astype(BF16)
+    send_ref[:, tall - 16:tall, :] = jnp.broadcast_to(tail[None], (near, 16, LANES))
 
 
 def coarse_partial_kernel(came_ref, send_ref):
     far, own, wide = send_ref.shape
-    d = wide - LANES
-    sums = jnp.sum(came_ref[...].astype(F32), axis=0)
-    send_ref[:, :, 0:d] = sums[:, 0:d].astype(BF16).reshape(far, own, d)
-    tail = tail_of(sums[:, d:d + 1] + sums[:, d + 1:d + 2])
-    send_ref[:, :, d:d + LANES] = tail.reshape(far, own, LANES)
+    rows, lane_blocks = far * own, wide // LANES - 1
+    for block in range(lane_blocks):
+        numer = jnp.sum(came_ref[:, block * rows:(block + 1) * rows, :].astype(F32), axis=0)
+        send_ref[:, :, block * LANES:(block + 1) * LANES] = numer.astype(BF16).reshape(far, own, LANES)
+    tail = jnp.sum(came_ref[:, lane_blocks * rows:lane_blocks * rows + 16, :].astype(F32), axis=0)
+    counts = jnp.where(lax.axis_index("xh") == 0, tail[0:1] + tail[2:3], tail[1:2] + tail[3:4])
+    column = jnp.broadcast_to(counts, (LANES, LANES)).T
+    column = jnp.where(lax.axis_index("zl") == 0, column[0:rows], column[rows:2 * rows])
+    send_ref[:, :, lane_blocks * LANES:wide] = tail_of(column[:, 0:1]).reshape(far, own, LANES)
 
 
 def new_coarse_kernel(core_ref, came_ref, mine_ref, send_ref):
@@ -258,11 +270,6 @@
     half_d, near_rows, own_rows = d // 2, rows // near, rows // (near * far)
     fine_t = fine_centroids.T
 
-    coarse_c, mine, core = call(
-        functools.partial(coarse_split_kernel, sizes),
-        (shape_of((2, rows, half_d), BF16), shape_of((own_rows, d), F32), shape_of((own_rows, LANES), jnp.int32)),
-        (), (coarse_centroids,),
-    )
     own = exchange(call(first_kernel, shape_of((groups, part, k), BF16), (), (fine_t,)), CHIPS)
     other = swap(own, "c")
     turned, rest, products, norms = call(
@@ -291,6 +298,12 @@
     new_fine_t, blocks = call(
         new_fine_kernel, (shape_of((part, k), F32), shape_of((groups, part, k), BF16)), (), (summed, fine_t)
     )
+    coarse_c, mine, core, new_fine_t = call(
+        functools.partial(coarse_split_kernel, sizes),
+        (shape_of((2, rows, half_d), BF16), shape_of((own_rows, d), F32), shape_of((own_rows, LANES), jnp.int32),
+         shape_of((part, k), F32)),
+        (), (coarse_centroids, new_fine_t),
+    )
     own = exchange(blocks, CHIPS)
     other = swap(own, "c")
     products = call(
@@ -304,7 +317,10 @@
     )
     lses = exchange(lses, ("c",) + CHIPS)
     wide = d + LANES
-    summed = call(coarse_numer_kernel, shape_of((near, near_rows, wide), BF16), (), (w, high, lses, own, other))
+    summed = call(
+        coarse_numer_kernel, shape_of((near, near_rows * d // LANES + 16, LANES), BF16),
+        (), (w, high, lses, own, other),
+    )
     summed = exchange(summed, NEAR)
     summed = exchange(call(coarse_partial_kernel, shape_of((far, own_rows, wide), BF16), (), (summed,)), "zh")
     blocks = call(new_coarse_kernel, shape_of((far, own_rows, d), BF16), (), (core, summed, mine))

time: 185 us -> 184 us (level)
  the two profiles are of different devices: /device:TPU:32 before, /device:TPU:8 now
where the time goes in v3:
time: 184 us
  blocking collectives  161 us (88%)
  Pallas kernels  11.4 us (6%)
  starting transfers between devices  5.74 us (3%)
  waiting for transfers between devices  3.29 us (2%)
    all_to_all x9, blocking collectives, exchange(): return lax.all_to_all(blocks, axis, split_axis=0, concat_axis=0, tiled=True)  161 us
    pallas_call x15, Pallas kernels, call(): pl.pallas_call(kernel, out_shape=out_shape, in_specs=specs, out_specs=out...  11.4 us
    ppermute x3, starting transfers between devices, swap(): return lax.ppermute(block, axis, PAIR)  5.74 us
  transfers between devices with their start and end apart: 3, of which 3 were waited for; matrix products, arithmetic and copies ran while one was open for 0% of the time, Pallas kernels for 3%

profile of v3, /device:TPU:8, one launch (start us, length us, event | category | flops | bytes accessed | tf_op | source)
XLA Modules:
  0.0 183.6 jit_solution(11707922852660096281)
XLA Ops:
  0.6 0.0 copy-start.1
  0.6 0.9 copy-done.1
  1.6 0.0 copy-start.3
  1.6 0.1 shard_map.50
  1.7 19.7 %all_to_all.45.own_ref = bf16[8,64,1024]{2,1,0:T(8,128)(2,1)S(1)} all-to-all(bf16[8,64,1024]{2,1,0:T(8,128)(2,1)S(1)} %shard_map.50), channel_id=1, replica_groups=mesh['y'=4,'xl'=2,'c'=2,'zh'=8,'zl'=2,'xh'=2] {'xl','y'}, dimensions={0} | all-to-all | bytes 2097152 | tf_op jit(solution)/shard_map/all_to_all | solution.py:43
  21.3 1.9 %collective-permute-start = (bf16[8,64,1024]{2,1,0:T(8,128)(2,1)S(1)}, bf16[8,64,1024]{2,1,0:T(8,128)(2,1)S(1)}, u32[]{:S(2)}, u32[]{:S(2)}) collective-permute-start(bf16[8,64,1024]{2,1,0:T(8,128)(2,1)S(1)} %all_to_all.45.own_ref), channel_id=1, source_target_pairs={{0,32},{32,0},{1,33},{33,1},{2,34},{34,2},{3,35},{35,3},{4,36},{36... | collective-permute-start | bytes 3145736 | tf_op jit(solution)/shard_map/ppermute | solution.py:47
  23.2 0.0 copy-done.3
  23.2 1.9 %shard_map.51 = (bf16[2,512,1024]{2,1,0:T(8,128)(2,1)S(1)}, bf16[1024,512]{1,0:T(8,128)(2,1)S(1)}, f32[1024,1024]{1,0:T(8,128)S(1)}, f32[1,1024]{1,0:T(1,128)S(1)}) custom-call(bf16[1024,1024]{1,0:T(8,128)(2,1)S(1)} %copy-done.3, bf16[8,64,1024]{2,1,0:T(8,128)(2,1)S(1)} %all_to_all.45.own_ref), custom_call_target="tpu_custom_call" | custom-call | flops 8589934592 | bytes 50331648 | tf_op jit(solution)/shard_map/pallas_call | solution.py:32
  25.2 0.7 collective-permute-done.other_ref
  25.9 2.1 %shard_map.52 = (bf16[1024,1024]{1,0:T(8,128)(2,1)S(1)}, f32[1,1024]{1,0:T(1,128)S(1)}, f32[32,1,1024]{2,1,0:T(1,128)S(1)}) custom-call(bf16[1024,512]{1,0:T(8,128)(2,1)S(1)} %get-tuple-element.21.points_ref, f32[1024,1024]{1,0:T(8,128)S(1)} %get-tuple-element.22.products_ref, f32[1,1024]{1,0:T(1,128)S(1)} %get-tuple-element.23.norms_ref, ...), custom_call_target="tpu_custom_call" | custom-call | tf_op jit(solution)/shard_map/pallas_call | solution.py:32
  28.0 34.8 %all_to_all.46.lses_ref = f32[32,1,1024]{2,1,0:T(1,128)S(1)} all-to-all(f32[32,1,1024]{2,1,0:T(1,128)S(1)} %get-tuple-element.26), channel_id=1, replica_groups=mesh['y'=4,'xl'=2,'c'=2,'zh'=8,'zl'=2,'xh'=2] {'xh','zl','zh'}, dimensions={0} | all-to-all | bytes 262144 | tf_op jit(solution)/shard_map/all_to_all | solution.py:43
  62.7 1.4 shard_map.53
  64.1 1.9 %collective-permute-start.1 = (bf16[528,1024]{1,0:T(8,128)(2,1)S(1)}, bf16[528,1024]{1,0:T(8,128)(2,1)S(1)}, u32[]{:S(2)}, u32[]{:S(2)}) collective-permute-start(bf16[528,1024]{1,0:T(8,128)(2,1)S(1)} %get-tuple-element.28.sent_ref), channel_id=1, source_target_pairs={{0,32},{32,0},{1,33},{33,1},{2,34},{34,2},{3,35},{35,3},{4,36},{36... | collective-permute-start | bytes 3244040 | tf_op jit(solution)/shard_map/ppermute | solution.py:47
  66.0 1.3 shard_map.54.keep_ref
  67.3 1.4 collective-permute-done.1.came_ref
  68.7 0.2 shard_map.55
  68.9 0.0 copy-start.2
  68.9 19.7 %all_to_all.47.came_ref = bf16[8,528,128]{2,1,0:T(8,128)(2,1)S(1)} all-to-all(bf16[8,528,128]{2,1,0:T(8,128)(2,1)S(1)} %shard_map.55), channel_id=1, replica_groups=mesh['y'=4,'xl'=2,'c'=2,'zh'=8,'zl'=2,'xh'=2] {'xl','y'}, dimensions={0} | all-to-all | bytes 2162688 | tf_op jit(solution)/shard_map/all_to_all | solution.py:43
  88.6 0.0 copy-done.2
  88.6 0.0 copy-start
  88.6 0.3 shard_map.56
  88.9 17.8 %all_to_all.48.own_ref = bf16[8,64,1024]{2,1,0:T(8,128)(2,1)S(1)} all-to-all(bf16[8,64,1024]{2,1,0:T(8,128)(2,1)S(1)} %get-tuple-element.33), channel_id=1, replica_groups=mesh['y'=4,'xl'=2,'c'=2,'zh'=8,'zl'=2,'xh'=2] {'xl','y'}, dimensions={0} | all-to-all | bytes 2097152 | tf_op jit(solution)/shard_map/all_to_all | solution.py:43
  106.7 1.9 %collective-permute-start.2 = (bf16[8,64,1024]{2,1,0:T(8,128)(2,1)S(1)}, bf16[8,64,1024]{2,1,0:T(8,128)(2,1)S(1)}, u32[]{:S(2)}, u32[]{:S(2)}) collective-permute-start(bf16[8,64,1024]{2,1,0:T(8,128)(2,1)S(1)} %all_to_all.48.own_ref), channel_id=1, source_target_pairs={{0,32},{32,0},{1,33},{33,1},{2,34},{34,2},{3,35},{35,3},{4,36},{36... | collective-permute-start | bytes 3145736 | tf_op jit(solution)/shard_map/ppermute | solution.py:47
  108.6 0.0 copy-done
  108.6 1.0 shard_map.57
  109.6 0.4 shard_map.58.products_ref
  110.1 1.2 collective-permute-done.2.other_ref
  111.3 0.6 shard_map.59
  111.9 9.1 %all_to_all.49.lses_ref = f32[16,1,1024]{2,1,0:T(1,128)S(1)} all-to-all(f32[16,1,1024]{2,1,0:T(1,128)S(1)} %get-tuple-element.36), channel_id=1, replica_groups=mesh['y'=4,'xl'=2,'c'=2,'zh'=8,'zl'=2,'xh'=2] {'c','xl','y'}, dimensions={0} | all-to-all | bytes 131072 | tf_op jit(solution)/shard_map/all_to_all | solution.py:43
  120.9 0.8 shard_map.60
  121.7 13.4 %all_to_all.50.came_ref = bf16[4,528,128]{2,1,0:T(8,128)(2,1)S(1)} all-to-all(bf16[4,528,128]{2,1,0:T(8,128)(2,1)S(1)} %shard_map.60), channel_id=1, replica_groups=mesh['y'=4,'xl'=2,'c'=2,'zh'=8,'zl'=2,'xh'=2] {'xh','zl'}, dimensions={0} | all-to-all | bytes 1081344 | tf_op jit(solution)/shard_map/all_to_all | solution.py:43
  135.1 0.2 shard_map.61
  135.3 19.0 %all_to_all.51.came_ref = bf16[8,8,1152]{2,1,0:T(8,128)(2,1)S(1)} all-to-all(bf16[8,8,1152]{2,1,0:T(8,128)(2,1)S(1)} %shard_map.61), channel_id=1, replica_groups=mesh['y'=4,'xl'=2,'c'=2,'zh'=8,'zl'=2,'xh'=2] {'zh'}, dimensions={0} | all-to-all | bytes 294912 | tf_op jit(solution)/shard_map/all_to_all | solution.py:43
  154.3 0.2 shard_map.62
  154.5 16.7 %all_to_all.52.came_ref = bf16[8,8,1024]{2,1,0:T(8,128)(2,1)S(1)} all-to-all(bf16[8,8,1024]{2,1,0:T(8,128)(2,1)S(1)} %shard_map.62), channel_id=1, replica_groups=mesh['y'=4,'xl'=2,'c'=2,'zh'=8,'zl'=2,'xh'=2] {'zh'}, dimensions={0} | all-to-all | bytes 262144 | tf_op jit(solution)/shard_map/all_to_all | solution.py:43
  171.2 11.4 %all_to_all.53.came_ref = bf16[4,64,1024]{2,1,0:T(8,128)(2,1)S(1)} all-to-all(bf16[4,64,1024]{2,1,0:T(8,128)(2,1)S(1)} %shard_map.63), channel_id=1, replica_groups=mesh['y'=4,'xl'=2,'c'=2,'zh'=8,'zl'=2,'xh'=2] {'xh','zl'}, dimensions={0} | all-to-all | bytes 1048576 | tf_op jit(solution)/shard_map/all_to_all | solution.py:43
  182.6 1.0 shard_map.64
  (1 shorter events, 0.0 us)
Async XLA Ops:
  0.6 1.0 copy-start.1
  1.6 21.6 %copy-start.3 = (bf16[1024,1024]{1,0:T(8,128)(2,1)S(1)}, bf16[1024,1024]{1,0:T(8,128)(2,1)}, u32[]{:S(2)}) copy-start(bf16[1024,1024]{1,0:T(8,128)(2,1)} %points_ref.1) | copy-start | bytes 6291460
  21.3 4.5 %collective-permute-start = (bf16[8,64,1024]{2,1,0:T(8,128)(2,1)S(1)}, bf16[8,64,1024]{2,1,0:T(8,128)(2,1)S(1)}, u32[]{:S(2)}, u32[]{:S(2)}) collective-permute-start(bf16[8,64,1024]{2,1,0:T(8,128)(2,1)S(1)} %all_to_all.45.own_ref), channel_id=1, source_target_pairs={{0,32},{32,0},{1,33},{33,1},{2,34},{34,2},{3,35},{35,3},{4,36},{36... | collective-permute-start | bytes 3145736 | tf_op jit(solution)/shard_map/ppermute | solution.py:47
  64.1 4.6 %collective-permute-start.1 = (bf16[528,1024]{1,0:T(8,128)(2,1)S(1)}, bf16[528,1024]{1,0:T(8,128)(2,1)S(1)}, u32[]{:S(2)}, u32[]{:S(2)}) collective-permute-start(bf16[528,1024]{1,0:T(8,128)(2,1)S(1)} %get-tuple-element.28.sent_ref), channel_id=1, source_target_pairs={{0,32},{32,0},{1,33},{33,1},{2,34},{34,2},{3,35},{35,3},{4,36},{36... | collective-permute-start | bytes 3244040 | tf_op jit(solution)/shard_map/ppermute | solution.py:47
  68.9 19.7 %copy-start.2 = (f32[1024,64]{0,1:T(8,128)S(1)}, f32[1024,64]{0,1:T(8,128)}, u32[]{:S(2)}) copy-start(f32[1024,64]{0,1:T(8,128)} %param.4) | copy-start | bytes 786436
  88.6 20.0 %copy-start = (f32[256,1024]{1,0:T(8,128)S(1)}, f32[256,1024]{1,0:T(8,128)}, u32[]{:S(2)}) copy-start(f32[256,1024]{1,0:T(8,128)} %coarse_ref.1) | copy-start | bytes 3145732
  106.7 4.5 %collective-permute-start.2 = (bf16[8,64,1024]{2,1,0:T(8,128)(2,1)S(1)}, bf16[8,64,1024]{2,1,0:T(8,128)(2,1)S(1)}, u32[]{:S(2)}, u32[]{:S(2)}) collective-permute-start(bf16[8,64,1024]{2,1,0:T(8,128)(2,1)S(1)} %all_to_all.48.own_ref), channel_id=1, source_target_pairs={{0,32},{32,0},{1,33},{33,1},{2,34},{34,2},{3,35},{35,3},{4,36},{36... | collective-permute-start | bytes 3145736 | tf_op jit(solution)/shard_map/ppermute | solution.py:47

commit v4 on v3

--- a/solution.py
+++ b/solution.py
@@ -88,7 +88,7 @@
     own = flat(own_ref)
     norms_ref[...] = norms_of(own)
     n = products_ref.shape[0]
-    tile = min(256, n)
+    tile = min(512, n)
     for start in range(0, n, tile):
         for at, columns in enumerate(by_core(points_ref[start:start + tile, :].T)):
             turned_ref[slots[at], :, start:start + tile] = columns
@@ -109,7 +109,7 @@
     other = flat(other_ref)
     norms = (norms_ref[...] + norms_of(other)) / scale
     n = products_ref.shape[0]
-    tile = min(256, n)
+    tile = min(512, n)
     for start in range(0, n, tile):
         products = products_ref[start:start + tile, :] + jnp.dot(
             points_ref[start:start + tile, :], other, preferred_element_type=F32
@@ -258,7 +258,16 @@
 
 
 def widen_kernel(came_ref, out_ref):
-    out_ref[...] = flat(came_ref).astype(F32)
+    out_ref[...] = came_ref[0].astype(F32)
+
+
+def widen(came):
+    near, rows, d = came.shape
+    return pl.pallas_call(
+        widen_kernel, grid=(near,), out_shape=shape_of((near * rows, d), F32), compiler_params=PARAMS,
+        in_specs=[pl.BlockSpec((1, rows, d), lambda at: (at, 0, 0))],
+        out_specs=pl.BlockSpec((rows, d), lambda at: (at, 0)),
+    )(came)
 
 
 def local(sizes, points, fine_centroids, coarse_centroids):
@@ -325,7 +334,7 @@
     summed = exchange(call(coarse_partial_kernel, shape_of((far, own_rows, wide), BF16), (), (summed,)), "zh")
     blocks = call(new_coarse_kernel, shape_of((far, own_rows, d), BF16), (), (core, summed, mine))
     blocks = call(repeat_kernel, shape_of((near, near_rows, d), BF16), (), (exchange(blocks, "zh"),))
-    new_coarse = call(widen_kernel, shape_of((rows, d), F32), (), (exchange(blocks, NEAR),))
+    new_coarse = widen(exchange(blocks, NEAR))
     return (new_fine_t.T, new_coarse)
 
 

time: 184 us -> 185 us (level)
    pallas_call x15 -> x14, Pallas kernels: 11.4 us -> 10.5 us  [call(): pl.pallas_call(kernel, out_shape=out_shape, in_specs=specs, out_specs=out...]
where the time goes in v4:
time: 185 us; the launch traced here: 184 us
  blocking collectives  161 us (87%)
  Pallas kernels  12 us (6%)
  starting transfers between devices  5.74 us (3%)
  waiting for transfers between devices  3.17 us (2%)
    all_to_all x9, blocking collectives, exchange(): return lax.all_to_all(blocks, axis, split_axis=0, concat_axis=0, tiled=True)  161 us
    pallas_call x14, Pallas kernels, call(): pl.pallas_call(kernel, out_shape=out_shape, in_specs=specs, out_specs=out...  10.5 us
    ppermute x3, starting transfers between devices, swap(): return lax.ppermute(block, axis, PAIR)  5.74 us
  transfers between devices with their start and end apart: 3, of which 3 were waited for; matrix products, arithmetic and copies ran while one was open for 0% of the time, Pallas kernels for 3%

profile of v4, /device:TPU:8, one launch (start us, length us, event | category | flops | bytes accessed | tf_op | source)
XLA Modules:
  0.0 184.1 jit_solution(7156516530403941927)
XLA Ops:
  0.6 0.0 copy-start.1
  0.6 0.9 copy-done.1
  1.6 0.0 copy-start.3
  1.6 0.1 shard_map.50
  1.7 19.7 %all_to_all.45.own_ref = bf16[8,64,1024]{2,1,0:T(8,128)(2,1)S(1)} all-to-all(bf16[8,64,1024]{2,1,0:T(8,128)(2,1)S(1)} %shard_map.50), channel_id=1, replica_groups=mesh['y'=4,'xl'=2,'c'=2,'zh'=8,'zl'=2,'xh'=2] {'xl','y'}, dimensions={0} | all-to-all | bytes 2097152 | tf_op jit(solution)/shard_map/all_to_all | solution.py:43
  21.3 1.9 %collective-permute-start = (bf16[8,64,1024]{2,1,0:T(8,128)(2,1)S(1)}, bf16[8,64,1024]{2,1,0:T(8,128)(2,1)S(1)}, u32[]{:S(2)}, u32[]{:S(2)}) collective-permute-start(bf16[8,64,1024]{2,1,0:T(8,128)(2,1)S(1)} %all_to_all.45.own_ref), channel_id=1, source_target_pairs={{0,32},{32,0},{1,33},{33,1},{2,34},{34,2},{3,35},{35,3},{4,36},{36... | collective-permute-start | bytes 3145736 | tf_op jit(solution)/shard_map/ppermute | solution.py:47
  23.2 0.0 copy-done.3
  23.2 2.1 %shard_map.51 = (bf16[2,512,1024]{2,1,0:T(8,128)(2,1)S(1)}, bf16[1024,512]{1,0:T(8,128)(2,1)S(1)}, f32[1024,1024]{1,0:T(8,128)S(1)}, f32[1,1024]{1,0:T(1,128)S(1)}) custom-call(bf16[1024,1024]{1,0:T(8,128)(2,1)S(1)} %copy-done.3, bf16[8,64,1024]{2,1,0:T(8,128)(2,1)S(1)} %all_to_all.45.own_ref), custom_call_target="tpu_custom_call" | custom-call | flops 8589934592 | bytes 50331648 | tf_op jit(solution)/shard_map/pallas_call | solution.py:32
  25.3 0.6 collective-permute-done.other_ref
  25.9 2.1 %shard_map.52 = (bf16[1024,1024]{1,0:T(8,128)(2,1)S(1)}, f32[1,1024]{1,0:T(1,128)S(1)}, f32[32,1,1024]{2,1,0:T(1,128)S(1)}) custom-call(bf16[1024,512]{1,0:T(8,128)(2,1)S(1)} %get-tuple-element.21.points_ref, f32[1024,1024]{1,0:T(8,128)S(1)} %get-tuple-element.22.products_ref, f32[1,1024]{1,0:T(1,128)S(1)} %get-tuple-element.23.norms_ref, ...), custom_call_target="tpu_custom_call" | custom-call | tf_op jit(solution)/shard_map/pallas_call | solution.py:32
  27.9 34.7 %all_to_all.46.lses_ref = f32[32,1,1024]{2,1,0:T(1,128)S(1)} all-to-all(f32[32,1,1024]{2,1,0:T(1,128)S(1)} %get-tuple-element.26), channel_id=1, replica_groups=mesh['y'=4,'xl'=2,'c'=2,'zh'=8,'zl'=2,'xh'=2] {'xh','zl','zh'}, dimensions={0} | all-to-all | bytes 262144 | tf_op jit(solution)/shard_map/all_to_all | solution.py:43
  62.7 1.4 shard_map.53
  64.1 1.9 %collective-permute-start.1 = (bf16[528,1024]{1,0:T(8,128)(2,1)S(1)}, bf16[528,1024]{1,0:T(8,128)(2,1)S(1)}, u32[]{:S(2)}, u32[]{:S(2)}) collective-permute-start(bf16[528,1024]{1,0:T(8,128)(2,1)S(1)} %get-tuple-element.28.sent_ref), channel_id=1, source_target_pairs={{0,32},{32,0},{1,33},{33,1},{2,34},{34,2},{3,35},{35,3},{4,36},{36... | collective-permute-start | bytes 3244040 | tf_op jit(solution)/shard_map/ppermute | solution.py:47
  66.0 1.3 shard_map.54.keep_ref
  67.2 1.4 collective-permute-done.1.came_ref
  68.7 0.2 shard_map.55
  68.9 0.0 copy-start.2
  68.9 19.7 %all_to_all.47.came_ref = bf16[8,528,128]{2,1,0:T(8,128)(2,1)S(1)} all-to-all(bf16[8,528,128]{2,1,0:T(8,128)(2,1)S(1)} %shard_map.55), channel_id=1, replica_groups=mesh['y'=4,'xl'=2,'c'=2,'zh'=8,'zl'=2,'xh'=2] {'xl','y'}, dimensions={0} | all-to-all | bytes 2162688 | tf_op jit(solution)/shard_map/all_to_all | solution.py:43
  88.6 0.0 copy-done.2
  88.6 0.0 copy-start
  88.6 0.3 shard_map.56
  88.9 17.8 %all_to_all.48.own_ref = bf16[8,64,1024]{2,1,0:T(8,128)(2,1)S(1)} all-to-all(bf16[8,64,1024]{2,1,0:T(8,128)(2,1)S(1)} %get-tuple-element.33), channel_id=1, replica_groups=mesh['y'=4,'xl'=2,'c'=2,'zh'=8,'zl'=2,'xh'=2] {'xl','y'}, dimensions={0} | all-to-all | bytes 2097152 | tf_op jit(solution)/shard_map/all_to_all | solution.py:43
  106.7 1.9 %collective-permute-start.2 = (bf16[8,64,1024]{2,1,0:T(8,128)(2,1)S(1)}, bf16[8,64,1024]{2,1,0:T(8,128)(2,1)S(1)}, u32[]{:S(2)}, u32[]{:S(2)}) collective-permute-start(bf16[8,64,1024]{2,1,0:T(8,128)(2,1)S(1)} %all_to_all.48.own_ref), channel_id=1, source_target_pairs={{0,32},{32,0},{1,33},{33,1},{2,34},{34,2},{3,35},{35,3},{4,36},{36... | collective-permute-start | bytes 3145736 | tf_op jit(solution)/shard_map/ppermute | solution.py:47
  108.6 0.0 copy-done
  108.6 1.0 shard_map.57
  109.6 0.4 shard_map.58.products_ref
  110.0 1.2 collective-permute-done.2.other_ref
  111.2 0.6 shard_map.59
  111.8 9.1 %all_to_all.49.lses_ref = f32[16,1,1024]{2,1,0:T(1,128)S(1)} all-to-all(f32[16,1,1024]{2,1,0:T(1,128)S(1)} %get-tuple-element.36), channel_id=1, replica_groups=mesh['y'=4,'xl'=2,'c'=2,'zh'=8,'zl'=2,'xh'=2] {'c','xl','y'}, dimensions={0} | all-to-all | bytes 131072 | tf_op jit(solution)/shard_map/all_to_all | solution.py:43
  120.9 0.8 shard_map.60
  121.7 13.4 %all_to_all.50.came_ref = bf16[4,528,128]{2,1,0:T(8,128)(2,1)S(1)} all-to-all(bf16[4,528,128]{2,1,0:T(8,128)(2,1)S(1)} %shard_map.60), channel_id=1, replica_groups=mesh['y'=4,'xl'=2,'c'=2,'zh'=8,'zl'=2,'xh'=2] {'xh','zl'}, dimensions={0} | all-to-all | bytes 1081344 | tf_op jit(solution)/shard_map/all_to_all | solution.py:43
  135.1 0.2 shard_map.61
  135.3 19.0 %all_to_all.51.came_ref = bf16[8,8,1152]{2,1,0:T(8,128)(2,1)S(1)} all-to-all(bf16[8,8,1152]{2,1,0:T(8,128)(2,1)S(1)} %shard_map.61), channel_id=1, replica_groups=mesh['y'=4,'xl'=2,'c'=2,'zh'=8,'zl'=2,'xh'=2] {'zh'}, dimensions={0} | all-to-all | bytes 294912 | tf_op jit(solution)/shard_map/all_to_all | solution.py:43
  154.3 0.2 shard_map.62
  154.5 16.7 %all_to_all.52.came_ref = bf16[8,8,1024]{2,1,0:T(8,128)(2,1)S(1)} all-to-all(bf16[8,8,1024]{2,1,0:T(8,128)(2,1)S(1)} %shard_map.62), channel_id=1, replica_groups=mesh['y'=4,'xl'=2,'c'=2,'zh'=8,'zl'=2,'xh'=2] {'zh'}, dimensions={0} | all-to-all | bytes 262144 | tf_op jit(solution)/shard_map/all_to_all | solution.py:43
  171.2 11.4 %all_to_all.53.came_ref = bf16[4,64,1024]{2,1,0:T(8,128)(2,1)S(1)} all-to-all(bf16[4,64,1024]{2,1,0:T(8,128)(2,1)S(1)} %shard_map.63), channel_id=1, replica_groups=mesh['y'=4,'xl'=2,'c'=2,'zh'=8,'zl'=2,'xh'=2] {'xh','zl'}, dimensions={0} | all-to-all | bytes 1048576 | tf_op jit(solution)/shard_map/all_to_all | solution.py:43
  182.5 1.5 shard_map.64
  (1 shorter events, 0.0 us)
Async XLA Ops:
  0.6 1.0 copy-start.1
  1.6 21.6 %copy-start.3 = (bf16[1024,1024]{1,0:T(8,128)(2,1)S(1)}, bf16[1024,1024]{1,0:T(8,128)(2,1)}, u32[]{:S(2)}) copy-start(bf16[1024,1024]{1,0:T(8,128)(2,1)} %points_ref.1) | copy-start | bytes 6291460
  21.3 4.5 %collective-permute-start = (bf16[8,64,1024]{2,1,0:T(8,128)(2,1)S(1)}, bf16[8,64,1024]{2,1,0:T(8,128)(2,1)S(1)}, u32[]{:S(2)}, u32[]{:S(2)}) collective-permute-start(bf16[8,64,1024]{2,1,0:T(8,128)(2,1)S(1)} %all_to_all.45.own_ref), channel_id=1, source_target_pairs={{0,32},{32,0},{1,33},{33,1},{2,34},{34,2},{3,35},{35,3},{4,36},{36... | collective-permute-start | bytes 3145736 | tf_op jit(solution)/shard_map/ppermute | solution.py:47
  64.1 4.6 %collective-permute-start.1 = (bf16[528,1024]{1,0:T(8,128)(2,1)S(1)}, bf16[528,1024]{1,0:T(8,128)(2,1)S(1)}, u32[]{:S(2)}, u32[]{:S(2)}) collective-permute-start(bf16[528,1024]{1,0:T(8,128)(2,1)S(1)} %get-tuple-element.28.sent_ref), channel_id=1, source_target_pairs={{0,32},{32,0},{1,33},{33,1},{2,34},{34,2},{3,35},{35,3},{4,36},{36... | collective-permute-start | bytes 3244040 | tf_op jit(solution)/shard_map/ppermute | solution.py:47
  68.9 19.7 %copy-start.2 = (f32[1024,64]{0,1:T(8,128)S(1)}, f32[1024,64]{0,1:T(8,128)}, u32[]{:S(2)}) copy-start(f32[1024,64]{0,1:T(8,128)} %param.4) | copy-start | bytes 786436
  88.6 20.0 %copy-start = (f32[256,1024]{1,0:T(8,128)S(1)}, f32[256,1024]{1,0:T(8,128)}, u32[]{:S(2)}) copy-start(f32[256,1024]{1,0:T(8,128)} %coarse_ref.1) | copy-start | bytes 3145732
  106.7 4.5 %collective-permute-start.2 = (bf16[8,64,1024]{2,1,0:T(8,128)(2,1)S(1)}, bf16[8,64,1024]{2,1,0:T(8,128)(2,1)S(1)}, u32[]{:S(2)}, u32[]{:S(2)}) collective-permute-start(bf16[8,64,1024]{2,1,0:T(8,128)(2,1)S(1)} %all_to_all.48.own_ref), channel_id=1, source_target_pairs={{0,32},{32,0},{1,33},{33,1},{2,34},{34,2},{3,35},{35,3},{4,36},{36... | collective-permute-start | bytes 3145736 | tf_op jit(solution)/shard_map/ppermute | solution.py:47

commit v5 on v3

--- a/solution.py
+++ b/solution.py
@@ -109,7 +109,7 @@
     other = flat(other_ref)
     norms = (norms_ref[...] + norms_of(other)) / scale
     n = products_ref.shape[0]
-    tile = min(256, n)
+    tile = min(128, n)
     for start in range(0, n, tile):
         products = products_ref[start:start + tile, :] + jnp.dot(
             points_ref[start:start + tile, :], other, preferred_element_type=F32

time: 184 us -> 184 us (level)
  no operation moved by 1% of the time
where the time goes in v5:
time: 184 us
  blocking collectives  161 us (88%)
  Pallas kernels  11.7 us (6%)
  starting transfers between devices  5.74 us (3%)
  waiting for transfers between devices  3.29 us (2%)
    all_to_all x9, blocking collectives, exchange(): return lax.all_to_all(blocks, axis, split_axis=0, concat_axis=0, tiled=True)  161 us
    pallas_call x15, Pallas kernels, call(): pl.pallas_call(kernel, out_shape=out_shape, in_specs=specs, out_specs=out...  11.7 us
    ppermute x3, starting transfers between devices, swap(): return lax.ppermute(block, axis, PAIR)  5.74 us
  transfers between devices with their start and end apart: 3, of which 3 were waited for; matrix products, arithmetic and copies ran while one was open for 0% of the time, Pallas kernels for 3%

profile of v5, /device:TPU:8, one launch (start us, length us, event | category | flops | bytes accessed | tf_op | source)
XLA Modules:
  0.0 183.9 jit_solution(10995703651409677154)
XLA Ops:
  0.6 0.0 copy-start.1
  0.6 0.9 copy-done.1
  1.6 0.0 copy-start.3
  1.6 0.1 shard_map.50
  1.7 19.7 %all_to_all.45.own_ref = bf16[8,64,1024]{2,1,0:T(8,128)(2,1)S(1)} all-to-all(bf16[8,64,1024]{2,1,0:T(8,128)(2,1)S(1)} %shard_map.50), channel_id=1, replica_groups=mesh['y'=4,'xl'=2,'c'=2,'zh'=8,'zl'=2,'xh'=2] {'xl','y'}, dimensions={0} | all-to-all | bytes 2097152 | tf_op jit(solution)/shard_map/all_to_all | solution.py:43
  21.3 1.9 %collective-permute-start = (bf16[8,64,1024]{2,1,0:T(8,128)(2,1)S(1)}, bf16[8,64,1024]{2,1,0:T(8,128)(2,1)S(1)}, u32[]{:S(2)}, u32[]{:S(2)}) collective-permute-start(bf16[8,64,1024]{2,1,0:T(8,128)(2,1)S(1)} %all_to_all.45.own_ref), channel_id=1, source_target_pairs={{0,32},{32,0},{1,33},{33,1},{2,34},{34,2},{3,35},{35,3},{4,36},{36... | collective-permute-start | bytes 3145736 | tf_op jit(solution)/shard_map/ppermute | solution.py:47
  23.2 0.0 copy-done.3
  23.2 1.9 %shard_map.51 = (bf16[2,512,1024]{2,1,0:T(8,128)(2,1)S(1)}, bf16[1024,512]{1,0:T(8,128)(2,1)S(1)}, f32[1024,1024]{1,0:T(8,128)S(1)}, f32[1,1024]{1,0:T(1,128)S(1)}) custom-call(bf16[1024,1024]{1,0:T(8,128)(2,1)S(1)} %copy-done.3, bf16[8,64,1024]{2,1,0:T(8,128)(2,1)S(1)} %all_to_all.45.own_ref), custom_call_target="tpu_custom_call" | custom-call | flops 8589934592 | bytes 50331648 | tf_op jit(solution)/shard_map/pallas_call | solution.py:32
  25.2 0.7 collective-permute-done.other_ref
  25.9 2.4 %shard_map.52 = (bf16[1024,1024]{1,0:T(8,128)(2,1)S(1)}, f32[1,1024]{1,0:T(1,128)S(1)}, f32[32,1,1024]{2,1,0:T(1,128)S(1)}) custom-call(bf16[1024,512]{1,0:T(8,128)(2,1)S(1)} %get-tuple-element.21.points_ref, f32[1024,1024]{1,0:T(8,128)S(1)} %get-tuple-element.22.products_ref, f32[1,1024]{1,0:T(1,128)S(1)} %get-tuple-element.23.norms_ref, ...), custom_call_target="tpu_custom_call" | custom-call | tf_op jit(solution)/shard_map/pallas_call | solution.py:32
  28.2 34.7 %all_to_all.46.lses_ref = f32[32,1,1024]{2,1,0:T(1,128)S(1)} all-to-all(f32[32,1,1024]{2,1,0:T(1,128)S(1)} %get-tuple-element.26), channel_id=1, replica_groups=mesh['y'=4,'xl'=2,'c'=2,'zh'=8,'zl'=2,'xh'=2] {'xh','zl','zh'}, dimensions={0} | all-to-all | bytes 262144 | tf_op jit(solution)/shard_map/all_to_all | solution.py:43
  62.9 1.4 shard_map.53
  64.3 1.9 %collective-permute-start.1 = (bf16[528,1024]{1,0:T(8,128)(2,1)S(1)}, bf16[528,1024]{1,0:T(8,128)(2,1)S(1)}, u32[]{:S(2)}, u32[]{:S(2)}) collective-permute-start(bf16[528,1024]{1,0:T(8,128)(2,1)S(1)} %get-tuple-element.28.sent_ref), channel_id=1, source_target_pairs={{0,32},{32,0},{1,33},{33,1},{2,34},{34,2},{3,35},{35,3},{4,36},{36... | collective-permute-start | bytes 3244040 | tf_op jit(solution)/shard_map/ppermute | solution.py:47
  66.2 1.3 shard_map.54.keep_ref
  67.5 1.4 collective-permute-done.1.came_ref
  68.9 0.2 shard_map.55
  69.1 0.0 copy-start.2
  69.1 19.7 %all_to_all.47.came_ref = bf16[8,528,128]{2,1,0:T(8,128)(2,1)S(1)} all-to-all(bf16[8,528,128]{2,1,0:T(8,128)(2,1)S(1)} %shard_map.55), channel_id=1, replica_groups=mesh['y'=4,'xl'=2,'c'=2,'zh'=8,'zl'=2,'xh'=2] {'xl','y'}, dimensions={0} | all-to-all | bytes 2162688 | tf_op jit(solution)/shard_map/all_to_all | solution.py:43
  88.9 0.0 copy-done.2
  88.9 0.0 copy-start
  88.9 0.3 shard_map.56
  89.2 17.8 %all_to_all.48.own_ref = bf16[8,64,1024]{2,1,0:T(8,128)(2,1)S(1)} all-to-all(bf16[8,64,1024]{2,1,0:T(8,128)(2,1)S(1)} %get-tuple-element.33), channel_id=1, replica_groups=mesh['y'=4,'xl'=2,'c'=2,'zh'=8,'zl'=2,'xh'=2] {'xl','y'}, dimensions={0} | all-to-all | bytes 2097152 | tf_op jit(solution)/shard_map/all_to_all | solution.py:43
  107.0 1.9 %collective-permute-start.2 = (bf16[8,64,1024]{2,1,0:T(8,128)(2,1)S(1)}, bf16[8,64,1024]{2,1,0:T(8,128)(2,1)S(1)}, u32[]{:S(2)}, u32[]{:S(2)}) collective-permute-start(bf16[8,64,1024]{2,1,0:T(8,128)(2,1)S(1)} %all_to_all.48.own_ref), channel_id=1, source_target_pairs={{0,32},{32,0},{1,33},{33,1},{2,34},{34,2},{3,35},{35,3},{4,36},{36... | collective-permute-start | bytes 3145736 | tf_op jit(solution)/shard_map/ppermute | solution.py:47
  108.9 0.0 copy-done
  108.9 1.0 shard_map.57
  109.9 0.4 shard_map.58.products_ref
  110.3 1.2 collective-permute-done.2.other_ref
  111.5 0.6 shard_map.59
  112.1 9.1 %all_to_all.49.lses_ref = f32[16,1,1024]{2,1,0:T(1,128)S(1)} all-to-all(f32[16,1,1024]{2,1,0:T(1,128)S(1)} %get-tuple-element.36), channel_id=1, replica_groups=mesh['y'=4,'xl'=2,'c'=2,'zh'=8,'zl'=2,'xh'=2] {'c','xl','y'}, dimensions={0} | all-to-all | bytes 131072 | tf_op jit(solution)/shard_map/all_to_all | solution.py:43
  121.2 0.8 shard_map.60
  122.0 13.4 %all_to_all.50.came_ref = bf16[4,528,128]{2,1,0:T(8,128)(2,1)S(1)} all-to-all(bf16[4,528,128]{2,1,0:T(8,128)(2,1)S(1)} %shard_map.60), channel_id=1, replica_groups=mesh['y'=4,'xl'=2,'c'=2,'zh'=8,'zl'=2,'xh'=2] {'xh','zl'}, dimensions={0} | all-to-all | bytes 1081344 | tf_op jit(solution)/shard_map/all_to_all | solution.py:43
  135.4 0.2 shard_map.61
  135.6 19.0 %all_to_all.51.came_ref = bf16[8,8,1152]{2,1,0:T(8,128)(2,1)S(1)} all-to-all(bf16[8,8,1152]{2,1,0:T(8,128)(2,1)S(1)} %shard_map.61), channel_id=1, replica_groups=mesh['y'=4,'xl'=2,'c'=2,'zh'=8,'zl'=2,'xh'=2] {'zh'}, dimensions={0} | all-to-all | bytes 294912 | tf_op jit(solution)/shard_map/all_to_all | solution.py:43
  154.6 0.2 shard_map.62
  154.7 16.7 %all_to_all.52.came_ref = bf16[8,8,1024]{2,1,0:T(8,128)(2,1)S(1)} all-to-all(bf16[8,8,1024]{2,1,0:T(8,128)(2,1)S(1)} %shard_map.62), channel_id=1, replica_groups=mesh['y'=4,'xl'=2,'c'=2,'zh'=8,'zl'=2,'xh'=2] {'zh'}, dimensions={0} | all-to-all | bytes 262144 | tf_op jit(solution)/shard_map/all_to_all | solution.py:43
  171.5 11.4 %all_to_all.53.came_ref = bf16[4,64,1024]{2,1,0:T(8,128)(2,1)S(1)} all-to-all(bf16[4,64,1024]{2,1,0:T(8,128)(2,1)S(1)} %shard_map.63), channel_id=1, replica_groups=mesh['y'=4,'xl'=2,'c'=2,'zh'=8,'zl'=2,'xh'=2] {'xh','zl'}, dimensions={0} | all-to-all | bytes 1048576 | tf_op jit(solution)/shard_map/all_to_all | solution.py:43
  182.8 1.0 shard_map.64
  (1 shorter events, 0.0 us)
Async XLA Ops:
  0.6 1.0 copy-start.1
  1.6 21.6 %copy-start.3 = (bf16[1024,1024]{1,0:T(8,128)(2,1)S(1)}, bf16[1024,1024]{1,0:T(8,128)(2,1)}, u32[]{:S(2)}) copy-start(bf16[1024,1024]{1,0:T(8,128)(2,1)} %points_ref.1) | copy-start | bytes 6291460
  21.3 4.5 %collective-permute-start = (bf16[8,64,1024]{2,1,0:T(8,128)(2,1)S(1)}, bf16[8,64,1024]{2,1,0:T(8,128)(2,1)S(1)}, u32[]{:S(2)}, u32[]{:S(2)}) collective-permute-start(bf16[8,64,1024]{2,1,0:T(8,128)(2,1)S(1)} %all_to_all.45.own_ref), channel_id=1, source_target_pairs={{0,32},{32,0},{1,33},{33,1},{2,34},{34,2},{3,35},{35,3},{4,36},{36... | collective-permute-start | bytes 3145736 | tf_op jit(solution)/shard_map/ppermute | solution.py:47
  64.3 4.6 %collective-permute-start.1 = (bf16[528,1024]{1,0:T(8,128)(2,1)S(1)}, bf16[528,1024]{1,0:T(8,128)(2,1)S(1)}, u32[]{:S(2)}, u32[]{:S(2)}) collective-permute-start(bf16[528,1024]{1,0:T(8,128)(2,1)S(1)} %get-tuple-element.28.sent_ref), channel_id=1, source_target_pairs={{0,32},{32,0},{1,33},{33,1},{2,34},{34,2},{3,35},{35,3},{4,36},{36... | collective-permute-start | bytes 3244040 | tf_op jit(solution)/shard_map/ppermute | solution.py:47
  69.1 19.8 %copy-start.2 = (f32[1024,64]{0,1:T(8,128)S(1)}, f32[1024,64]{0,1:T(8,128)}, u32[]{:S(2)}) copy-start(f32[1024,64]{0,1:T(8,128)} %param.4) | copy-start | bytes 786436
  88.9 20.0 %copy-start = (f32[256,1024]{1,0:T(8,128)S(1)}, f32[256,1024]{1,0:T(8,128)}, u32[]{:S(2)}) copy-start(f32[256,1024]{1,0:T(8,128)} %coarse_ref.1) | copy-start | bytes 3145732
  107.0 4.5 %collective-permute-start.2 = (bf16[8,64,1024]{2,1,0:T(8,128)(2,1)S(1)}, bf16[8,64,1024]{2,1,0:T(8,128)(2,1)S(1)}, u32[]{:S(2)}, u32[]{:S(2)}) collective-permute-start(bf16[8,64,1024]{2,1,0:T(8,128)(2,1)S(1)} %all_to_all.48.own_ref), channel_id=1, source_target_pairs={{0,32},{32,0},{1,33},{33,1},{2,34},{34,2},{3,35},{35,3},{4,36},{36... | collective-permute-start | bytes 3145736 | tf_op jit(solution)/shard_map/ppermute | solution.py:47
